TPU v7x, 128 devices: a whole 4x4x4 slice. The times are simulated.
128 devices in a mesh: front: 4 (over x), row: 4 (over z), col: 8 (over y, core).
Axes of the slice: x: 4, y: 4, z: 4, core: 2. Of those that a mesh axis runs over, the one named last changes fastest.
Arguments:
- tiles: float32 [4096, 256, 256], P(('front', 'row', 'col')), may hold values from -6 to 6
- dest: int32 [4096, 1], P(('front', 'row', 'col')), may hold values from 0 to 15; in each aligned block of 32 rows (0 to 31, 32 to 63, ...) at most 4 rows name the same one
- block_row: int32 [4096], P(('front', 'row', 'col')), may hold values from 0 to 9
- block_col: int32 [4096], P(('front', 'row', 'col')), may hold values from 0 to 4
- rows_from: int32 [4096, 256], P(('front', 'row', 'col')), may hold values from 0 to 255, each once within a row
- cols_from: int32 [4096, 256], P(('front', 'row', 'col')), may hold values from 0 to 255, each once within a row
- initial: float32 [4, 10240, 512], P('front', 'row', 'col'), may hold values from -6 to 60, as said below
- pattern: int32 [4, 2, 40], P('front'), may hold values 0 or 1
Outputs:
- factored: float32 [4, 10240, 10240], P('front', 'row', 'col')
Inputs may be any that keep to these rules, and one draw needn't show every extreme that they name: `dest`: in the rows of one device no destination is named by more than 4 tiles, a bound that some block reaches. `rows_from`: each row is a permutation. `cols_from`: each row is a permutation. `initial`: the first 512 rows form a symmetric block whose diagonal entries exceed the sum of magnitudes of the other entries in their rows.
All inputs are finite; a program needn't handle non-finite values. No bound on the sum of `pattern` on one device may be relied on, other than what follows from the above.
Results may differ from a plain program's by a relative error of at most 0.0001.
Values sent between devices are 32-bit elements; how exact they have to be, the bound alone decides.
No kernel may reach another device: no remote copies, remote signals or barrier semaphores. Data moves between devices by JAX's collectives and lax.ppermute only.
A program may use at most 192 MiB of HBM per device.

v0:
```python
import jax
import jax.numpy as jnp
from jax import lax
from jax.experimental import pallas as pl
from jax.experimental.pallas import tpu as pltpu
from jax.sharding import PartitionSpec as P

ORDER = 10240
BS = 256
CAP = 4
PIV = 512
STRIP = 32
NSTRIP = BS // STRIP
NCHIP = NSTRIP // 2
MARK = 8
PARTS = (64, 96, 96)
OFFSETS = tuple(sum(PARTS[:q]) for q in range(len(PARTS)))
NPART = len(PARTS)
GROUP = 8
RING = 8

HIGH = lax.Precision.HIGHEST
f32, bf16, i32 = jnp.float32, jnp.bfloat16, jnp.int32


def lower_sym(block):
    return jnp.tril(block) + jnp.tril(block, -1).T


def permute_kernel(slot_ref, label_ref, tile_ref, rows_ref, cols_ref, *refs):
    chip_refs, part_refs = refs[:NCHIP], refs[NCHIP : NCHIP + NPART]
    hold, mark, mark_sem, strip_sems, part_sems = refs[NCHIP + NPART :]
    step = pl.program_id(0)

    def marks():
        rows = part_refs[0].at[:, pl.ds(PARTS[0], MARK)]
        return pltpu.make_async_copy(mark, rows, mark_sem)

    @pl.when(step == 0)
    def _():
        def fill(s, carry):
            mark[s] = jnp.full(mark.shape[1:], label_ref[s].astype(f32))
            return carry

        lax.fori_loop(0, mark.shape[0], fill, 0)
        marks().start()

    half = BS // 2
    lane = lax.broadcasted_iota(i32, (BS, half), 1)
    place = lax.broadcasted_iota(i32, (BS, BS), 0)

    def move(g, carry):
        t = step * GROUP + g
        tile = tile_ref[g]
        high = tile.astype(bf16)
        rest = tile - high.astype(f32)
        mid = rest.astype(bf16)
        low = (rest - mid.astype(f32)).astype(bf16)
        parts = jnp.concatenate([high, mid, low], axis=1)
        wanted = jnp.transpose(jnp.broadcast_to(rows_ref[g], (half, BS)))
        pick_rows = jnp.concatenate(
            [jnp.where(wanted == lane + k * half, 1.0, 0.0) for k in range(2)], axis=1
        ).astype(bf16)
        pick_cols = jnp.where(place == cols_ref[g], 1.0, 0.0).astype(bf16)
        moved = jnp.dot(pick_rows, parts, preferred_element_type=f32).astype(bf16)
        out = jnp.dot(moved[:, :BS], pick_cols, preferred_element_type=f32)
        out = out + jnp.dot(moved[:, BS : 2 * BS], pick_cols, preferred_element_type=f32)
        out = out + jnp.dot(moved[:, 2 * BS :], pick_cols, preferred_element_type=f32)
        hold[t] = out
        for k in range(NSTRIP):
            pltpu.make_async_copy(
                hold.at[t, pl.ds(k * STRIP, STRIP)], chip_refs[k // 2].at[k % 2, t], strip_sems.at[t]
            ).start()
        for q in range(NPART):
            pltpu.make_async_copy(
                hold.at[t, pl.ds(OFFSETS[q], PARTS[q])],
                part_refs[q].at[slot_ref[t], pl.ds(0, PARTS[q])],
                part_sems.at[t],
            ).start()
        return carry

    lax.fori_loop(0, GROUP, move, 0, unroll=2)

    @pl.when(step == pl.num_programs(0) - 1)
    def _():
        def finish(t, carry):
            pltpu.make_async_copy(hold.at[t], hold.at[t], strip_sems.at[t]).wait()
            pltpu.make_async_copy(hold.at[t], hold.at[t], part_sems.at[t]).wait()
            return carry

        lax.fori_loop(0, hold.shape[0], finish, 0)
        marks().wait()


def permute(slot, labels, tiles, rows_from, cols_from, slots):
    count = tiles.shape[0]
    out = pl.pallas_call(
        permute_kernel,
        grid_spec=pltpu.PrefetchScalarGridSpec(
            num_scalar_prefetch=2,
            grid=(count // GROUP,),
            in_specs=[
                pl.BlockSpec((GROUP, BS, BS), lambda t, slot, labels: (t, 0, 0)),
                pl.BlockSpec((GROUP, 1, BS), lambda t, slot, labels: (t, 0, 0)),
                pl.BlockSpec((GROUP, 1, BS), lambda t, slot, labels: (t, 0, 0)),
            ],
            out_specs=[pl.BlockSpec(memory_space=pl.ANY)] * (NCHIP + NPART),
            scratch_shapes=[
                pltpu.VMEM((count, BS, BS), f32),
                pltpu.VMEM((slots, MARK, BS), f32),
                pltpu.SemaphoreType.DMA(()),
                pltpu.SemaphoreType.DMA((count,)),
                pltpu.SemaphoreType.DMA((count,)),
            ],
        ),
        out_shape=[jax.ShapeDtypeStruct((2, count, STRIP, BS), f32)] * NCHIP
        + [
            jax.ShapeDtypeStruct((slots, n + (MARK if q == 0 else 0), BS), f32)
            for q, n in enumerate(PARTS)
        ],
        compiler_params=pltpu.CompilerParams(vmem_limit_bytes=58 << 20),
        cost_estimate=pl.CostEstimate(
            flops=12 * count * BS**3, bytes_accessed=12 * count * BS * BS, transcendentals=0
        ),
        name="permute_tiles",
    )(slot, labels, tiles, rows_from[:, None, :], cols_from[:, None, :])
    return list(out[:NCHIP]), list(out[NCHIP:])


def slot_kernel(count, meta, own_ref, other_ref, out_ref, hold, in_sem, sems):
    @pl.when(meta[count] % 2 == 0)
    def _():
        copy = pltpu.make_async_copy(own_ref.at[0], hold, in_sem)
        copy.start()
        copy.wait()

    @pl.when(meta[count] % 2 == 1)
    def _():
        copy = pltpu.make_async_copy(other_ref, hold, in_sem)
        copy.start()
        copy.wait()

    def begin(t, carry):
        pltpu.make_async_copy(hold.at[t], out_ref.at[meta[t]], sems.at[t]).start()
        return carry

    lax.fori_loop(0, count, begin, 0)

    def finish(t, carry):
        pltpu.make_async_copy(hold.at[t], out_ref.at[meta[t]], sems.at[t]).wait()
        return carry

    lax.fori_loop(0, count, finish, 0)


def slot_strips(meta, own, other, slots):
    count = other.shape[0]
    return pl.pallas_call(
        lambda *refs: slot_kernel(count, *refs),
        grid_spec=pltpu.PrefetchScalarGridSpec(
            num_scalar_prefetch=1,
            grid=(1,),
            in_specs=[pl.BlockSpec(memory_space=pl.ANY)] * 2,
            out_specs=pl.BlockSpec(memory_space=pl.ANY),
            scratch_shapes=[
                pltpu.VMEM(other.shape, f32),
                pltpu.SemaphoreType.DMA(()),
                pltpu.SemaphoreType.DMA((count,)),
            ],
        ),
        out_shape=jax.ShapeDtypeStruct((slots, STRIP, BS), f32),
        compiler_params=pltpu.CompilerParams(vmem_limit_bytes=58 << 20),
        cost_estimate=pl.CostEstimate(
            flops=0, bytes_accessed=8 * count * STRIP * BS, transcendentals=0
        ),
        name="slot_strips",
    )(meta, own, other)


def slab_kernel(meta, initial_ref, in_ref, out_ref, ring, sems):
    total = meta[128]
    pieces, width = initial_ref.shape[0], initial_ref.shape[3]

    def copy(g):
        return pltpu.make_async_copy(in_ref.at[meta[g]], ring.at[g % RING], sems.at[g % RING])

    for g in range(RING):

        @pl.when(g < total)
        def _():
            copy(g).start()

    for k in range(pieces):
        out_ref[:, :, k * width : (k + 1) * width] = initial_ref[k]

    @pl.loop(0, total)
    def _(g):
        copy(g).wait()
        spot = meta[64 + g]
        cols = pl.ds(pl.multiple_of((spot % 2) * BS, BS), BS)
        out_ref[spot // 2, :, cols] += ring[g % RING]

        @pl.when(g + RING < total)
        def _():
            copy(g + RING).start()


def slab_strip(meta, initial, incoming):
    pieces, blocks, height, width = initial.shape
    shape = (blocks, height, pieces * width)
    return pl.pallas_call(
        slab_kernel,
        grid_spec=pltpu.PrefetchScalarGridSpec(
            num_scalar_prefetch=1,
            grid=(1,),
            in_specs=[
                pl.BlockSpec(initial.shape, lambda i, meta: (0, 0, 0, 0)),
                pl.BlockSpec(memory_space=pl.ANY),
            ],
            out_specs=pl.BlockSpec(shape, lambda i, meta: (0, 0, 0)),
            scratch_shapes=[
                pltpu.VMEM((RING, height, BS), f32),
                pltpu.SemaphoreType.DMA((RING,)),
            ],
        ),
        out_shape=jax.ShapeDtypeStruct(shape, f32),
        compiler_params=pltpu.CompilerParams(vmem_limit_bytes=32 << 20),
        cost_estimate=pl.CostEstimate(
            flops=0, bytes_accessed=12 * blocks * STRIP * PIV, transcendentals=0
        ),
        name="slab_strip",
    )(meta, initial, incoming)


def halves(x):
    high = x.astype(bf16)
    return high, (x - high.astype(f32)).astype(bf16)


def final_kernel(col_blocks, *refs):
    meta = refs[0]
    slab, first_factor, second_factor = refs[1:4]
    across, incoming = refs[4], refs[5 : 5 + NPART]
    out_ref, a_high, a_low, ring, sems = refs[5 + NPART :]
    b = pl.program_id(0)
    total = meta[138]

    def copies(g):
        return [
            pltpu.make_async_copy(
                incoming[q].at[meta[g], pl.ds(0, PARTS[q])],
                ring.at[g % RING, pl.ds(OFFSETS[q], PARTS[q])],
                sems.at[g % RING, q],
            )
            for q in range(NPART)
        ]

    @pl.when(b == 0)
    def _():
        for g in range(RING):

            @pl.when(g < total)
            def _():
                for c in copies(g):
                    c.start()

        for cb in range(col_blocks):
            high, low = halves(across[:, cb].reshape(BS, PIV).T)
            a_high[:, cb * BS : (cb + 1) * BS] = high
            a_low[:, cb * BS : (cb + 1) * BS] = low

    rows = slab[:, 0].reshape(BS, PIV)
    top = meta[139] == 1
    high, low = halves(jnp.where(jnp.logical_and(top, b < 2), 0.0, rows))
    for cb in range(col_blocks):
        cols = slice(cb * BS, (cb + 1) * BS)
        product = jnp.dot(high, a_low[:, cols], preferred_element_type=f32)
        product = product + jnp.dot(low, a_high[:, cols], preferred_element_type=f32)
        product = product + jnp.dot(high, a_high[:, cols], preferred_element_type=f32)
        out_ref[:, cols] = -product

    @pl.loop(meta[128 + b], meta[129 + b])
    def _(g):
        for c in copies(g):
            c.wait()
        cols = pl.ds(pl.multiple_of(meta[64 + g] * BS, BS), BS)
        out_ref[:, cols] += ring[g % RING]

        @pl.when(g + RING < total)
        def _():
            for c in copies(g + RING):
                c.start()

    @pl.when(meta[140] == 0)
    def _():
        out_ref[:, :BS] = jnp.where(jnp.logical_and(top, b == 0), first_factor[...], rows[:, :BS])
        out_ref[:, BS:PIV] = jnp.where(jnp.logical_and(top, b == 1), second_factor[...], rows[:, BS:])


def final(meta, slab, across, mats, incoming, row_blocks, col_blocks):
    whole = pl.BlockSpec((BS, BS), lambda b, meta: (0, 0))
    return pl.pallas_call(
        lambda *refs: final_kernel(col_blocks, *refs),
        grid_spec=pltpu.PrefetchScalarGridSpec(
            num_scalar_prefetch=1,
            grid=(row_blocks,),
            in_specs=[
                pl.BlockSpec((NSTRIP, 1, STRIP, PIV), lambda b, meta: (0, b, 0, 0)),
            ]
            + [whole] * 2
            + [pl.BlockSpec((NSTRIP, col_blocks, STRIP, PIV), lambda b, meta: (0, 0, 0, 0))]
            + [pl.BlockSpec(memory_space=pl.ANY)] * NPART,
            out_specs=pl.BlockSpec((BS, col_blocks * BS), lambda b, meta: (b, 0)),
            scratch_shapes=[
                pltpu.VMEM((PIV, col_blocks * BS), bf16),
                pltpu.VMEM((PIV, col_blocks * BS), bf16),
                pltpu.VMEM((RING, BS, BS), f32),
                pltpu.SemaphoreType.DMA((RING, NPART)),
            ],
        ),
        out_shape=jax.ShapeDtypeStruct((row_blocks * BS, col_blocks * BS), f32),
        compiler_params=pltpu.CompilerParams(vmem_limit_bytes=48 << 20),
        cost_estimate=pl.CostEstimate(
            flops=6 * row_blocks * col_blocks * BS * BS * PIV,
            bytes_accessed=4 * 2 * row_blocks * col_blocks * BS * BS,
            transcendentals=0,
        ),
        name="place_and_update",
    )(meta, slab, *mats, across, *incoming)


def dot(a, b):
    return jnp.dot(a, b, precision=HIGH)


def inverse(lower):
    size = lower.shape[0]
    eye = jnp.eye(size, dtype=f32)
    scale = jnp.sum(lower * eye, axis=0)
    power = eye - lower / scale[None, :]
    out = eye + power
    for _ in range(6):
        power = dot(power, power)
        out = out + dot(power, out)
    return out / scale[:, None]


def panel(block):
    half = BS // 2
    first = jnp.linalg.cholesky(lower_sym(block[:half, :half]))
    first_inv = inverse(first)
    below = dot(block[half:, :half], first_inv.T)
    second = jnp.linalg.cholesky(lower_sym(block[half:, half:] - dot(below, below.T)))
    second_inv = inverse(second)
    across = -dot(second_inv, dot(below, first_inv))
    zero = jnp.zeros((half, half), f32)
    factor = jnp.block([[first, zero], [below, second]])
    return factor, jnp.block([[first_inv.T, across.T], [zero, second_inv.T]])


def exchange(x, my_col, n_col):
    chip, core = my_col // 2, my_col % 2
    chips = n_col // 2
    pairs = x
    got = []
    for step in range(chips):
        pair = lax.dynamic_index_in_dim(pairs, (chip + step) % chips, 0, keepdims=False)
        if step:
            pair = lax.ppermute(pair, "col", [(c, (c + 2 * step) % n_col) for c in range(n_col)])
        got.append(pair)

    def from_chips(wanted):
        ordered_by = [lax.dynamic_index_in_dim(p, wanted, 0, keepdims=False) for p in got]
        return jnp.stack(ordered_by)

    mine = from_chips(core)
    other = lax.ppermute(from_chips(1 - core), "col", [(c, c ^ 1) for c in range(n_col)])
    both = jnp.stack([jnp.where(core == 0, mine, other), jnp.where(core == 0, other, mine)], 1)
    placed = [
        lax.dynamic_index_in_dim(both, (chip + chips - k) % chips, 0, keepdims=False)
        for k in range(chips)
    ]
    return jnp.stack(placed).reshape((n_col,) + x.shape[2:])


def ordered(key, valid, span):
    count = key.shape[0]
    key = jnp.where(valid, key, span)
    index = jnp.arange(count, dtype=i32)
    ahead = (key[None, :] < key[:, None]) | (
        (key[None, :] == key[:, None]) & (index[None, :] < index[:, None])
    )
    rank = jnp.sum(ahead.astype(i32), axis=1)
    chosen = rank[None, :] == index[:, None]
    order = jnp.sum(jnp.where(chosen, index[None, :], 0), axis=1)
    return order, jnp.sum(jnp.where(chosen, key[None, :], 0), axis=1), key


def body(tiles, dest, block_row, block_col, rows_from, cols_from, initial, pattern):
    n_front = lax.axis_size("front")
    n_row = lax.axis_size("row")
    n_col = lax.axis_size("col")
    my_row = lax.axis_index("row")
    my_col = lax.axis_index("col")
    row_blocks = ORDER // n_row // BS
    col_blocks = ORDER // n_col // BS
    lead = PIV // BS
    slots = n_front * n_row * CAP
    target = dest[:, 0]
    owner_row = target % n_row
    local_row = jnp.where(owner_row == 0, lead + block_row % (row_blocks - lead), block_row)
    block_id = local_row * col_blocks + block_col
    same = (target[:, None] == target[None, :]).astype(i32)
    slot = target * CAP + jnp.sum(jnp.tril(same, -1), axis=1)
    choose = jnp.arange(slots, dtype=i32)[:, None] == slot[None, :]
    labels = jnp.where(
        jnp.any(choose, axis=1), jnp.sum(jnp.where(choose, block_id[None, :], 0), axis=1), -1
    )
    pivot = initial[0, :PIV]
    sent = [lax.ppermute(pivot, "row", [(0, to)]) for to in range(1, n_row)]
    pivot = jnp.where(my_row == 0, pivot, sent[0] + sent[1] + sent[2])
    row = jnp.zeros((1, pivot.shape[1]), f32).at[0, : slot.shape[0]].set(slot.astype(f32))
    near = jnp.concatenate([pivot, jnp.broadcast_to(row, (8, row.shape[1]))])
    near, slot = lax.optimization_barrier((near, slot))
    near = lax.all_gather(near, "col", axis=0)
    corner = near[:, :PIV].transpose(1, 0, 2).reshape(PIV, PIV)
    slot_meta = jnp.append(near[0, PIV, : slot.shape[0]].astype(i32), my_col)

    def send(part):
        return lax.all_to_all(part, ("front", "row"), split_axis=0, concat_axis=0, tiled=True)

    strips, parts = permute(slot, labels, tiles, rows_from, cols_from, slots)
    incoming = [send(parts[0])]
    got = [lax.ppermute(strips[k], "col", [(0, 2 * k)]) for k in range(1, NCHIP)]
    own = jnp.where(my_col == 0, strips[0], got[0] + got[1] + got[2])
    other = lax.ppermute(own[1], "col", [(2 * k, 2 * k + 1) for k in range(NCHIP)])
    first, first_inv = panel(corner[:BS, :BS])
    below = dot(corner[BS:, :BS], first_inv)
    below = jnp.where(pattern[0, 0, 1] == 1, below, jnp.zeros_like(below))
    rest = corner[BS:, BS:] - dot(below, below.T)
    second, second_inv = panel(rest)
    cross = dot(below.T, second_inv)
    other, first, second, first_inv, second_inv, cross = lax.optimization_barrier(
        (other, first, second, first_inv, second_inv, cross)
    )
    slotted = slot_strips(slot_meta, own, other, slots)
    slotted, incoming[0] = lax.optimization_barrier((slotted, incoming[0]))
    names = incoming[0][:, PARTS[0], 0]
    pivot_columns = initial[0].reshape(row_blocks, NSTRIP, STRIP, -1).transpose(1, 0, 2, 3)
    pivot_columns = pivot_columns.reshape(NCHIP, 2, row_blocks * STRIP, -1)
    extra = jnp.broadcast_to(names, (NCHIP, 2, 8, slots))
    got = exchange(jnp.concatenate([pivot_columns, extra], axis=2), my_col, n_col)
    pivot_columns = got[:, : row_blocks * STRIP].reshape(n_col, row_blocks, STRIP, -1)
    first_names = got[0, row_blocks * STRIP].astype(i32)
    names = names.astype(i32)

    valid = names >= 0
    order, sorted_id, key = ordered(names, valid, row_blocks * col_blocks)
    bounds = jnp.arange(row_blocks + 1, dtype=i32)[:, None] * col_blocks
    starts = jnp.sum((key[None, :] < bounds).astype(i32), axis=1)
    in_slab = (first_names >= 0) & (first_names % col_blocks < lead)
    slab_key = (first_names // col_blocks) * lead + first_names % col_blocks
    slab_order, slab_id, _ = ordered(slab_key, in_slab, row_blocks * lead)
    slab_meta = jnp.concatenate(
        [slab_order, slab_id, jnp.sum(in_slab.astype(i32))[None], my_col[None]]
    )

    meta = jnp.concatenate(
        [order, sorted_id % col_blocks, starts, (my_row == 0).astype(i32)[None], my_col[None]]
    )

    strip = slab_strip(slab_meta, pivot_columns, send(slotted))

    blocks = my_row * row_blocks + jnp.arange(row_blocks, dtype=i32)
    flags = lax.dynamic_slice_in_dim(pattern[0], my_row * row_blocks, row_blocks, 1)
    keep = (flags == 1) & (blocks[None, :] > jnp.arange(2, dtype=i32)[:, None])
    keep = jnp.repeat(keep, STRIP, axis=1)[:, :, None]
    strip = strip.reshape(row_blocks * STRIP, PIV)
    one = dot(strip[:, :BS], first_inv)
    one = jnp.where(keep[0], one, jnp.zeros_like(one))
    two = dot(strip[:, BS:], second_inv) - dot(one, cross)
    two = jnp.where(keep[1], two, jnp.zeros_like(two))
    solved = jnp.concatenate([one, two], axis=1).reshape(row_blocks, STRIP, PIV)

    part, solved = lax.optimization_barrier((parts[1], solved))
    rows = lax.all_gather(solved, "row", axis=0)
    incoming.append(send(part))
    part, rows, solved, incoming[1] = lax.optimization_barrier((parts[2], rows, solved, incoming[1]))
    incoming.append(send(part))
    slab = lax.all_gather(solved, "col", axis=0)
    across = exchange(rows.reshape(NCHIP, 2, col_blocks, STRIP, PIV), my_col, n_col)
    return final(meta, slab, across, (first, second), incoming, row_blocks, col_blocks)[None]


def solution(mesh):
    placed = (
        P(("front", "row", "col"), None, None),
        P(("front", "row", "col"), None),
        P(("front", "row", "col")),
        P(("front", "row", "col")),
        P(("front", "row", "col"), None),
        P(("front", "row", "col"), None),
        P("front", "row", "col"),
        P("front", None, None),
    )
    return jax.shard_map(
        body, mesh=mesh, in_specs=placed, out_specs=P("front", "row", "col"), check_vma=False
    )
```

profile of v0, /device:TPU:124, one launch (start us, length us, event | category | flops | bytes accessed | tf_op | source)
XLA Modules:
  0.0 444.1 jit_solution(13190270108516591177)
XLA Ops:
  13.0 2.8 collective-permute-done.2
  23.0 16.8 %permute_tiles.1 = (f32[2,32,32,256]{3,2,1,0:T(8,128)}, f32[2,32,32,256]{3,2,1,0:T(8,128)}, f32[2,32,32,256]{3,2,1,0:T(8,128)}, f32[2,32,32,256]{3,2,1,0:T(8,128...) custom-call(s32[32]{0:T(128)} %copy-done.13, s32[64]{0:T(128)} %broadcast_select_fusion.1.label_ref, ...), custom_call_target="tpu_custom_call" | custom-call | flops 6442450944 | bytes 25165824 | tf_op jit(solution)/shard_map/permute_tiles/pallas_call | solution.py:97
  39.8 9.8 %all-to-all-start = ((f32[64,72,256]{2,1,0:T(8,128)}), f32[64,72,256]{2,1,0:T(8,128)}, u32[]{:S(2)}, u32[]{:S(2)}) async-start(f32[64,72,256]{2,1,0:T(8,128)} %get-tuple-element.48), calls=%async_computation | async-start | bytes 9437184 | tf_op jit(solution)/shard_map/all_to_all | solution.py:430
  49.6 2.1 collective-permute-start.3
  56.8 11.7 %cholesky.74 = f32[128,128]{1,0:T(8,128)S(1)} custom-call(f32[128,128]{1,0:T(8,128)S(1)} %copy.211), custom_call_target="Cholesky" | custom-call | tf_op jit(solution)/shard_map/jit(cholesky)/cholesky | solution.py:350
  73.3 11.7 %cholesky.85 = f32[128,128]{1,0:T(8,128)S(1)} custom-call(f32[128,128]{1,0:T(8,128)S(1)} %copy.216), custom_call_target="Cholesky" | custom-call | tf_op jit(solution)/shard_map/jit(cholesky)/cholesky | solution.py:353
  91.1 11.7 %cholesky.96 = f32[128,128]{1,0:T(8,128)S(1)} custom-call(f32[128,128]{1,0:T(8,128)S(1)} %copy.228), custom_call_target="Cholesky" | custom-call | tf_op jit(solution)/shard_map/jit(cholesky)/cholesky | solution.py:350
  109.0 11.7 %cholesky.107 = f32[128,128]{1,0:T(8,128)S(1)} custom-call(f32[128,128]{1,0:T(8,128)S(1)} %fusion.25), custom_call_target="Cholesky" | custom-call | tf_op jit(solution)/shard_map/jit(cholesky)/cholesky | solution.py:353
  126.2 4.1 add_select_fusion.refs_1_
  130.4 2.3 collective-permute-start.6
  135.9 3.2 slot_strips.1
  143.2 7.2 %all-to-all-start.1 = ((f32[64,32,256]{2,1,0:T(8,128)}), f32[64,32,256]{2,1,0:T(8,128)S(1)}, u32[]{:S(2)}, u32[]{:S(2)}) async-start(f32[64,32,256]{2,1,0:T(8,128)} %slot_strips.1), calls=%async_computation.1 | async-start | bytes 4194304 | tf_op jit(solution)/shard_map/all_to_all | solution.py:430
  152.2 6.7 %collective-permute-start.8 = (f32[2,328,64]{1,2,0:T(8,128)}, f32[2,328,64]{1,2,0:T(8,128)}, u32[]{:S(2)}, u32[]{:S(2)}) collective-permute-start(f32[2,328,64]{1,2,0:T(8,128)} %bitcast.228), channel_id=1, source_target_pairs={{0,4},{1,5},{2,6},{3,7},{4,0},{5,1},{6,2},{7,3},{8,12},{9,13},{10,... | collective-permute-start | bytes 503816 | tf_op jit(solution)/shard_map/ppermute | solution.py:369
  163.8 3.7 collective-permute-done.7
  181.0 6.9 %all-to-all-start.2 = ((f32[64,96,256]{2,1,0:T(8,128)}), f32[64,96,256]{2,1,0:T(8,128)}, u32[]{:S(2)}, u32[]{:S(2)}) async-start(f32[64,96,256]{2,1,0:T(8,128)} %get-tuple-element.57), calls=%async_computation.2 | async-start | bytes 12582912 | tf_op jit(solution)/shard_map/all_to_all | solution.py:430
  188.7 112.0 %all-gather.8.cloned.1.call-done = f32[40,32,512]{2,1,0:T(8,128)} async-done(((f32[10,32,512]{2,1,0:T(8,128)}), f32[40,32,512]{2,1,0:T(8,128)}) %all-gather.8.cloned.1.call-update) | async-done | bytes 2621456 | tf_op jit(solution)/shard_map/all_gather | solution.py:486
  300.8 7.1 %all-to-all-start.3 = ((f32[64,96,256]{2,1,0:T(8,128)}), f32[64,96,256]{2,1,0:T(8,128)}, u32[]{:S(2)}, u32[]{:S(2)}) async-start(f32[64,96,256]{2,1,0:T(8,128)} %get-tuple-element.63), calls=%async_computation.3 | async-start | bytes 12582912 | tf_op jit(solution)/shard_map/all_to_all | solution.py:430
  308.2 2.0 collective-permute-start.13
  310.2 26.1 %collective-permute-done.11 = f32[2,5,32,512]{3,2,1,0:T(8,128)S(1)} collective-permute-done((f32[2,5,32,512]{3,2,1,0:T(8,128)S(1)}, f32[2,5,32,512]{3,2,1,0:T(8,128)S(1)}, u32[]{:S(2)}, u32[]{:S(2)}) %collective-permute-start.11) | collective-permute-done | bytes 655392 | tf_op jit(solution)/shard_map/ppermute | solution.py:369
  336.4 14.9 %collective-permute-done.13 = f32[2,5,32,512]{3,2,1,0:T(8,128)S(1)} collective-permute-done((f32[2,5,32,512]{3,2,1,0:T(8,128)S(1)}, f32[2,5,32,512]{3,2,1,0:T(8,128)S(1)}, u32[]{:S(2)}, u32[]{:S(2)}) %collective-permute-start.13) | collective-permute-done | bytes 655392 | tf_op jit(solution)/shard_map/ppermute | solution.py:369
  352.1 6.6 %collective-permute-done.12 = f32[2,5,32,512]{3,2,1,0:T(8,128)S(1)} collective-permute-done((f32[2,5,32,512]{3,2,1,0:T(8,128)S(1)}, f32[2,5,32,512]{3,2,1,0:T(8,128)S(1)}, u32[]{:S(2)}, u32[]{:S(2)}) %collective-permute-start.12) | collective-permute-done | bytes 655392 | tf_op jit(solution)/shard_map/ppermute | solution.py:369
  360.3 2.4 collective-permute-done.14
  364.9 53.1 %all-to-all-done.3.refs_7_ = f32[64,96,256]{2,1,0:T(8,128)} async-done(((f32[64,96,256]{2,1,0:T(8,128)}), f32[64,96,256]{2,1,0:T(8,128)}, u32[]{:S(2)}, u32[]{:S(2)}) %all-to-all-start.3) | async-done | bytes 6291488 | tf_op jit(solution)/shard_map/all_to_all | solution.py:430
  418.0 19.1 %place_and_update.1 = f32[2560,1280]{1,0:T(8,128)} custom-call(s32[141]{0:T(256)S(1)} %concatenate.74.refs_0_, f32[8,10,32,512]{3,2,1,0:T(8,128)} %bitcast.205, f32[256,256]{1,0:T(8,128)S(1)} %copy-done, f32[256,256]{1,0:T(8,128)S(1)} %copy-done.1, f32[8,5,32,512]{3,2,1,0:T(8,128)S(1)} %bitcast.196, f32[64,72,256]{2,1,0:T(8,128)} %all-to-all-done.refs_5_, ...), custom_call_target="tpu_custom_call" | custom-call | flops 10066329600 | bytes 26214400 | tf_op jit(solution)/shard_map/place_and_update/pallas_call | solution.py:302
  (239 shorter events, 72.7 us)
Async XLA Ops:
  6.5 48.6 %all-gather.12.cloned.1.call-start = ((), (), s32[]{:S(2)}) async-start(), calls=%async_computation.6 | async-start | bytes 1474560 | tf_op jit(solution)/shard_map/all_gather | solution.py:425
  7.5 8.3 %collective-permute-start.2 = (f32[512,64]{0,1:T(8,128)S(1)}, f32[512,64]{0,1:T(8,128)S(1)}, u32[]{:S(2)}, u32[]{:S(2)}) collective-permute-start(f32[512,64]{0,1:T(8,128)S(1)} %slice_bitcast_fusion.1), channel_id=1, source_target_pairs={{0,24},{1,25},{2,26},{3,27},{4,28},{5,29},{6,30},{7,31},{32,56},{3... | collective-permute-start | bytes 393224 | tf_op jit(solution)/shard_map/ppermute | solution.py:420
  8.8 7.0 %collective-permute-start.1 = (f32[512,64]{0,1:T(8,128)S(1)}, f32[512,64]{0,1:T(8,128)S(1)}, u32[]{:S(2)}, u32[]{:S(2)}) collective-permute-start(f32[512,64]{0,1:T(8,128)S(1)} %slice_bitcast_fusion.1), channel_id=1, source_target_pairs={{0,16},{1,17},{2,18},{3,19},{4,20},{5,21},{6,22},{7,23},{32,48},{3... | collective-permute-start | bytes 393224 | tf_op jit(solution)/shard_map/ppermute | solution.py:420
  9.5 6.4 %collective-permute-start = (f32[512,64]{0,1:T(8,128)S(1)}, f32[512,64]{0,1:T(8,128)S(1)}, u32[]{:S(2)}, u32[]{:S(2)}) collective-permute-start(f32[512,64]{0,1:T(8,128)S(1)} %slice_bitcast_fusion.1), channel_id=1, source_target_pairs={{0,8},{1,9},{2,10},{3,11},{4,12},{5,13},{6,14},{7,15},{32,40},{33,... | collective-permute-start | bytes 393224 | tf_op jit(solution)/shard_map/ppermute | solution.py:420
  39.8 99.3 %all-to-all-start = ((f32[64,72,256]{2,1,0:T(8,128)}), f32[64,72,256]{2,1,0:T(8,128)}, u32[]{:S(2)}, u32[]{:S(2)}) async-start(f32[64,72,256]{2,1,0:T(8,128)} %get-tuple-element.48), calls=%async_computation | async-start | bytes 9437184 | tf_op jit(solution)/shard_map/all_to_all | solution.py:430
  49.6 76.5 %collective-permute-start.3 = (f32[2,32,32,256]{3,2,1,0:T(8,128)}, f32[2,32,32,256]{3,2,1,0:T(8,128)}, u32[]{:S(2)}, u32[]{:S(2)}) collective-permute-start(f32[2,32,32,256]{3,2,1,0:T(8,128)} %get-tuple-element.44), channel_id=1, source_target_pairs={{0,2},{8,10},{16,18},{24,26},{32,34},{40,42},{48,50},{56,58},{64,6... | collective-permute-start | bytes 6291464 | tf_op jit(solution)/shard_map/ppermute | solution.py:434
  51.7 74.5 %collective-permute-start.4 = (f32[2,32,32,256]{3,2,1,0:T(8,128)}, f32[2,32,32,256]{3,2,1,0:T(8,128)}, u32[]{:S(2)}, u32[]{:S(2)}) collective-permute-start(f32[2,32,32,256]{3,2,1,0:T(8,128)} %get-tuple-element.45), channel_id=1, source_target_pairs={{0,4},{8,12},{16,20},{24,28},{32,36},{40,44},{48,52},{56,60},{64,6... | collective-permute-start | bytes 6291464 | tf_op jit(solution)/shard_map/ppermute | solution.py:434
  53.7 72.5 %collective-permute-start.5 = (f32[2,32,32,256]{3,2,1,0:T(8,128)}, f32[2,32,32,256]{3,2,1,0:T(8,128)}, u32[]{:S(2)}, u32[]{:S(2)}) collective-permute-start(f32[2,32,32,256]{3,2,1,0:T(8,128)} %get-tuple-element.46), channel_id=1, source_target_pairs={{0,6},{8,14},{16,22},{24,30},{32,38},{40,46},{48,54},{56,62},{64,7... | collective-permute-start | bytes 6291464 | tf_op jit(solution)/shard_map/ppermute | solution.py:434
  130.4 5.5 %collective-permute-start.6 = (f32[32,32,256]{2,1,0:T(8,128)S(1)}, f32[32,32,256]{2,1,0:T(8,128)}, u32[]{:S(2)}, u32[]{:S(2)}) collective-permute-start(f32[32,32,256]{2,1,0:T(8,128)S(1)} %slice_bitcast_fusion), channel_id=1, source_target_pairs={{0,1},{2,3},{4,5},{6,7},{8,9},{10,11},{12,13},{14,15},{16,17},{18,... | collective-permute-start | bytes 3145736 | tf_op jit(solution)/shard_map/ppermute | solution.py:436
  142.4 19.5 %collective-permute-start.9 = (f32[2,328,64]{1,2,0:T(8,128)}, f32[2,328,64]{1,2,0:T(8,128)}, u32[]{:S(2)}, u32[]{:S(2)}) collective-permute-start(f32[2,328,64]{1,2,0:T(8,128)} %bitcast.30), channel_id=1, source_target_pairs={{0,6},{1,7},{2,0},{3,1},{4,2},{5,3},{6,4},{7,5},{8,14},{9,15},{10,... | collective-permute-start | bytes 503816 | tf_op jit(solution)/shard_map/ppermute | solution.py:369
  143.2 33.7 %all-to-all-start.1 = ((f32[64,32,256]{2,1,0:T(8,128)}), f32[64,32,256]{2,1,0:T(8,128)S(1)}, u32[]{:S(2)}, u32[]{:S(2)}) async-start(f32[64,32,256]{2,1,0:T(8,128)} %slot_strips.1), calls=%async_computation.1 | async-start | bytes 4194304 | tf_op jit(solution)/shard_map/all_to_all | solution.py:430
  152.2 10.7 %collective-permute-start.8 = (f32[2,328,64]{1,2,0:T(8,128)}, f32[2,328,64]{1,2,0:T(8,128)}, u32[]{:S(2)}, u32[]{:S(2)}) collective-permute-start(f32[2,328,64]{1,2,0:T(8,128)} %bitcast.228), channel_id=1, source_target_pairs={{0,4},{1,5},{2,6},{3,7},{4,0},{5,1},{6,2},{7,3},{8,12},{9,13},{10,... | collective-permute-start | bytes 503816 | tf_op jit(solution)/shard_map/ppermute | solution.py:369
  161.8 5.7 %collective-permute-start.7 = (f32[2,328,64]{1,2,0:T(8,128)S(1)}, f32[2,328,64]{1,2,0:T(8,128)S(1)}, u32[]{:S(2)}, u32[]{:S(2)}) collective-permute-start(f32[2,328,64]{1,2,0:T(8,128)S(1)} %bitcast.229), channel_id=1, source_target_pairs={{0,2},{1,3},{2,4},{3,5},{4,6},{5,7},{6,0},{7,1},{8,10},{9,11},{10,... | collective-permute-start | bytes 503816 | tf_op jit(solution)/shard_map/ppermute | solution.py:369
  167.6 1.9 collective-permute-start.10
  181.0 119.8 %all-to-all-start.2 = ((f32[64,96,256]{2,1,0:T(8,128)}), f32[64,96,256]{2,1,0:T(8,128)}, u32[]{:S(2)}, u32[]{:S(2)}) async-start(f32[64,96,256]{2,1,0:T(8,128)} %get-tuple-element.57), calls=%async_computation.2 | async-start | bytes 12582912 | tf_op jit(solution)/shard_map/all_to_all | solution.py:430
  187.9 112.8 %all-gather.8.cloned.1.call-start = ((), (), s32[]{:S(2)}) async-start(), calls=%async_computation.4 | async-start | bytes 3276800 | tf_op jit(solution)/shard_map/all_gather | solution.py:486
  188.7 229.3 %all-gather.10.cloned.1.call-start = ((), (), s32[]{:S(2)}) async-start(), calls=%async_computation.5 | async-start | bytes 5898240 | tf_op jit(solution)/shard_map/all_gather | solution.py:490
  300.8 117.2 %all-to-all-start.3 = ((f32[64,96,256]{2,1,0:T(8,128)}), f32[64,96,256]{2,1,0:T(8,128)}, u32[]{:S(2)}, u32[]{:S(2)}) async-start(f32[64,96,256]{2,1,0:T(8,128)} %get-tuple-element.63), calls=%async_computation.3 | async-start | bytes 12582912 | tf_op jit(solution)/shard_map/all_to_all | solution.py:430
  308.1 28.3 %collective-permute-start.11 = (f32[2,5,32,512]{3,2,1,0:T(8,128)S(1)}, f32[2,5,32,512]{3,2,1,0:T(8,128)S(1)}, u32[]{:S(2)}, u32[]{:S(2)}) collective-permute-start(f32[2,5,32,512]{3,2,1,0:T(8,128)S(1)} %get-tuple-element.90), channel_id=1, source_target_pairs={{0,2},{1,3},{2,4},{3,5},{4,6},{5,7},{6,0},{7,1},{8,10},{9,11},{10,... | collective-permute-start | bytes 1966088 | tf_op jit(solution)/shard_map/ppermute | solution.py:369
  308.2 43.2 %collective-permute-start.13 = (f32[2,5,32,512]{3,2,1,0:T(8,128)S(1)}, f32[2,5,32,512]{3,2,1,0:T(8,128)S(1)}, u32[]{:S(2)}, u32[]{:S(2)}) collective-permute-start(f32[2,5,32,512]{3,2,1,0:T(8,128)S(1)} %get-tuple-element.91), channel_id=1, source_target_pairs={{0,6},{1,7},{2,0},{3,1},{4,2},{5,3},{6,4},{7,5},{8,14},{9,15},{10,... | collective-permute-start | bytes 1966088 | tf_op jit(solution)/shard_map/ppermute | solution.py:369
  310.2 48.5 %collective-permute-start.12 = (f32[2,5,32,512]{3,2,1,0:T(8,128)S(1)}, f32[2,5,32,512]{3,2,1,0:T(8,128)S(1)}, u32[]{:S(2)}, u32[]{:S(2)}) collective-permute-start(f32[2,5,32,512]{3,2,1,0:T(8,128)S(1)} %get-tuple-element.92), channel_id=1, source_target_pairs={{0,4},{1,5},{2,6},{3,7},{4,0},{5,1},{6,2},{7,3},{8,12},{9,13},{10,... | collective-permute-start | bytes 1966088 | tf_op jit(solution)/shard_map/ppermute | solution.py:369
  359.6 3.1 collective-permute-start.14
  364.6 53.4 %copy-start = (f32[256,256]{1,0:T(8,128)S(1)}, f32[256,256]{1,0:T(8,128)}, u32[]{:S(2)}) copy-start(f32[256,256]{1,0:T(8,128)} %select_maximum_fusion.3.refs_2_) | copy-start | bytes 786436
  364.6 53.4 %copy-start.1 = (f32[256,256]{1,0:T(8,128)S(1)}, f32[256,256]{1,0:T(8,128)}, u32[]{:S(2)}) copy-start(f32[256,256]{1,0:T(8,128)} %select_maximum_fusion.1.refs_3_) | copy-start | bytes 786436
  (14 other events, 96.8 us)
Sparse Core Ops, SparseCore 0:
  17.7 26.1 all-gather.11
  190.4 110.2 all-gather.7
  302.5 60.5 all-gather.9
where the time goes:
time: 448 us; the launch traced here: 444 us
  waiting for transfers between devices  224 us (50%)
  other arithmetic  76.5 us (17%)
  starting transfers between devices  51.3 us (11%)
  Pallas kernels  40.9 us (9%)
  local copies, waits for them, and re-layouts  20.5 us (5%)
  matrix products  15.7 us (4%)
  between operations  15.5 us (3%)
    all_gather x1, waiting for transfers between devices, body(): rows = lax.all_gather(solved, 'row', axis=0)  112 us
    all_to_all x4, waiting for transfers between devices, send(): lax.all_to_all(part, ('front', 'row'), split_axis=0, concat_axis=0, tiled...  53.1 us
    ppermute x6, waiting for transfers between devices, exchange(): lax.ppermute(pair, 'col', [(c, (c + 2 * step) % n_col) for c in range(n_c...  51.3 us
    all_to_all x4, starting transfers between devices, send(): lax.all_to_all(part, ('front', 'row'), split_axis=0, concat_axis=0, tiled...  31 us
    another operation x6, other arithmetic, panel(): jnp.linalg.cholesky(lower_sym(block[half:, half:] - dot(below, below.T)))  24.9 us
    another operation x6, other arithmetic, panel(): first = jnp.linalg.cholesky(lower_sym(block[:half, :half]))  24.8 us
    pallas_call x1, Pallas kernels, final(): pl.pallas_call(lambda *refs: final_kernel(col_blocks, *refs), grid_spec=p...  19.1 us
    pallas_call x1, Pallas kernels, permute(): pl.pallas_call(permute_kernel, grid_spec=pltpu.PrefetchScalarGridSpec(num...  16.8 us
  transfers between devices with their start and end apart: 22, of which 9 were waited for; matrix products, arithmetic and copies ran while one was open for 23% of the time, Pallas kernels for 5%

commit v1 on v0

--- a/solution.py
+++ b/solution.py
@@ -13,7 +13,7 @@
 NSTRIP = BS // STRIP
 NCHIP = NSTRIP // 2
 MARK = 8
-PARTS = (64, 96, 96)
+PARTS = (96, 80, 80)
 OFFSETS = tuple(sum(PARTS[:q]) for q in range(len(PARTS)))
 NPART = len(PARTS)
 GROUP = 8
@@ -416,21 +416,20 @@
     labels = jnp.where(
         jnp.any(choose, axis=1), jnp.sum(jnp.where(choose, block_id[None, :], 0), axis=1), -1
     )
-    pivot = initial[0, :PIV]
+    def send(part):
+        return lax.all_to_all(part, ("front", "row"), split_axis=0, concat_axis=0, tiled=True)
+
+    strips, parts = permute(slot, labels, tiles, rows_from, cols_from, slots)
+    incoming = [send(parts[0])]
+    strips[0], pivot, slot = lax.optimization_barrier((strips[0], initial[0, :PIV], slot))
     sent = [lax.ppermute(pivot, "row", [(0, to)]) for to in range(1, n_row)]
     pivot = jnp.where(my_row == 0, pivot, sent[0] + sent[1] + sent[2])
     row = jnp.zeros((1, pivot.shape[1]), f32).at[0, : slot.shape[0]].set(slot.astype(f32))
     near = jnp.concatenate([pivot, jnp.broadcast_to(row, (8, row.shape[1]))])
-    near, slot = lax.optimization_barrier((near, slot))
+    near, *strips = lax.optimization_barrier((near, *strips))
     near = lax.all_gather(near, "col", axis=0)
     corner = near[:, :PIV].transpose(1, 0, 2).reshape(PIV, PIV)
     slot_meta = jnp.append(near[0, PIV, : slot.shape[0]].astype(i32), my_col)
-
-    def send(part):
-        return lax.all_to_all(part, ("front", "row"), split_axis=0, concat_axis=0, tiled=True)
-
-    strips, parts = permute(slot, labels, tiles, rows_from, cols_from, slots)
-    incoming = [send(parts[0])]
     got = [lax.ppermute(strips[k], "col", [(0, 2 * k)]) for k in range(1, NCHIP)]
     own = jnp.where(my_col == 0, strips[0], got[0] + got[1] + got[2])
     other = lax.ppermute(own[1], "col", [(2 * k, 2 * k + 1) for k in range(NCHIP)])
@@ -438,11 +437,7 @@
     below = dot(corner[BS:, :BS], first_inv)
     below = jnp.where(pattern[0, 0, 1] == 1, below, jnp.zeros_like(below))
     rest = corner[BS:, BS:] - dot(below, below.T)
-    second, second_inv = panel(rest)
-    cross = dot(below.T, second_inv)
-    other, first, second, first_inv, second_inv, cross = lax.optimization_barrier(
-        (other, first, second, first_inv, second_inv, cross)
-    )
+    other, first, first_inv, rest = lax.optimization_barrier((other, first, first_inv, rest))
     slotted = slot_strips(slot_meta, own, other, slots)
     slotted, incoming[0] = lax.optimization_barrier((slotted, incoming[0]))
     names = incoming[0][:, PARTS[0], 0]
@@ -471,24 +466,29 @@
 
     strip = slab_strip(slab_meta, pivot_columns, send(slotted))
 
-    blocks = my_row * row_blocks + jnp.arange(row_blocks, dtype=i32)
-    flags = lax.dynamic_slice_in_dim(pattern[0], my_row * row_blocks, row_blocks, 1)
-    keep = (flags == 1) & (blocks[None, :] > jnp.arange(2, dtype=i32)[:, None])
+    part, strip, rest = lax.optimization_barrier((parts[1], strip, rest))
+    incoming.append(send(part))
+    rows = lax.all_gather(strip, "row", axis=0)
+    second, second_inv = panel(rest)
+    cross = dot(below.T, second_inv)
+    part, rows, incoming[1], second, second_inv, cross = lax.optimization_barrier(
+        (parts[2], rows, incoming[1], second, second_inv, cross)
+    )
+    incoming.append(send(part))
+
+    blocks = jnp.arange(n_row * row_blocks, dtype=i32)
+    keep = (pattern[0] == 1) & (blocks[None, :] > jnp.arange(2, dtype=i32)[:, None])
     keep = jnp.repeat(keep, STRIP, axis=1)[:, :, None]
-    strip = strip.reshape(row_blocks * STRIP, PIV)
-    one = dot(strip[:, :BS], first_inv)
+    rows = rows.reshape(n_row * row_blocks * STRIP, PIV)
+    one = dot(rows[:, :BS], first_inv)
     one = jnp.where(keep[0], one, jnp.zeros_like(one))
-    two = dot(strip[:, BS:], second_inv) - dot(one, cross)
+    two = dot(rows[:, BS:], second_inv) - dot(one, cross)
     two = jnp.where(keep[1], two, jnp.zeros_like(two))
-    solved = jnp.concatenate([one, two], axis=1).reshape(row_blocks, STRIP, PIV)
-
-    part, solved = lax.optimization_barrier((parts[1], solved))
-    rows = lax.all_gather(solved, "row", axis=0)
-    incoming.append(send(part))
-    part, rows, solved, incoming[1] = lax.optimization_barrier((parts[2], rows, solved, incoming[1]))
-    incoming.append(send(part))
-    slab = lax.all_gather(solved, "col", axis=0)
-    across = exchange(rows.reshape(NCHIP, 2, col_blocks, STRIP, PIV), my_col, n_col)
+    solved = jnp.concatenate([one, two], axis=1).reshape(n_row, row_blocks, STRIP, PIV)
+    slab = lax.all_gather(
+        lax.dynamic_index_in_dim(solved, my_row, 0, keepdims=False), "col", axis=0
+    )
+    across = exchange(solved.reshape(NCHIP, 2, col_blocks, STRIP, PIV), my_col, n_col)
     return final(meta, slab, across, (first, second), incoming, row_blocks, col_blocks)[None]
 
 

time: 448 us -> 435 us (0.971)
  the two profiles are of different devices: /device:TPU:124 before, /device:TPU:7 now
where the time goes in v1:
time: 435 us; the launch traced here: 430 us
  waiting for transfers between devices  185 us (43%)
  other arithmetic  76.2 us (18%)
  starting transfers between devices  65.2 us (15%)
  Pallas kernels  42.1 us (10%)
  local copies, waits for them, and re-layouts  26.1 us (6%)
  matrix products  19.6 us (5%)
  between operations  15.2 us (3%)
    all_gather x1, waiting for transfers between devices, body(): rows = lax.all_gather(strip, 'row', axis=0)  61.4 us
    all_to_all x4, waiting for transfers between devices, send(): lax.all_to_all(part, ('front', 'row'), split_axis=0, concat_axis=0, tiled...  56 us
    ppermute x6, waiting for transfers between devices, exchange(): lax.ppermute(pair, 'col', [(c, (c + 2 * step) % n_col) for c in range(n_c...  50.7 us
    all_to_all x4, starting transfers between devices, send(): lax.all_to_all(part, ('front', 'row'), split_axis=0, concat_axis=0, tiled...  33.5 us
    another operation x6, other arithmetic, panel(): first = jnp.linalg.cholesky(lower_sym(block[:half, :half]))  24.8 us
    another operation x6, other arithmetic, panel(): jnp.linalg.cholesky(lower_sym(block[half:, half:] - dot(below, below.T)))  24.8 us
    dot_general x62, matrix products, dot(): return jnp.dot(a, b, precision=HIGH)  19.6 us
    pallas_call x1, Pallas kernels, final(): pl.pallas_call(lambda *refs: final_kernel(col_blocks, *refs), grid_spec=p...  19.2 us
  transfers between devices with their start and end apart: 22, of which 13 were waited for; matrix products, arithmetic and copies ran while one was open for 20% of the time, Pallas kernels for 1%

profile of v1, /device:TPU:7, one launch (start us, length us, event | category | flops | bytes accessed | tf_op | source)
XLA Modules:
  0.0 429.6 jit_solution(8813861675474702680)
XLA Ops:
  12.6 16.9 %permute_tiles.1 = (f32[2,32,32,256]{3,2,1,0:T(8,128)}, f32[2,32,32,256]{3,2,1,0:T(8,128)}, f32[2,32,32,256]{3,2,1,0:T(8,128)}, f32[2,32,32,256]{3,2,1,0:T(8,128...) custom-call(s32[32]{0:T(128)} %copy-done.11, s32[64]{0:T(128)} %broadcast_select_fusion.1.label_ref, ...), custom_call_target="tpu_custom_call" | custom-call | flops 6442450944 | bytes 25165824 | tf_op jit(solution)/shard_map/permute_tiles/pallas_call | solution.py:97
  29.4 5.7 %collective-permute-start.2 = (f32[512,64]{0,1:T(8,128)S(1)}, f32[512,64]{0,1:T(8,128)S(1)}, u32[]{:S(2)}, u32[]{:S(2)}) collective-permute-start(f32[512,64]{0,1:T(8,128)S(1)} %slice_bitcast_fusion.1), channel_id=1, source_target_pairs={{0,24},{1,25},{2,26},{3,27},{4,28},{5,29},{6,30},{7,31},{32,56},{3... | collective-permute-start | bytes 393224 | tf_op jit(solution)/shard_map/ppermute | solution.py:425
  42.2 6.3 %all-to-all-start = ((f32[64,104,256]{2,1,0:T(8,128)}), f32[64,104,256]{2,1,0:T(8,128)}, u32[]{:S(2)}, u32[]{:S(2)}) async-start(f32[64,104,256]{2,1,0:T(8,128)} %get-tuple-element.61), calls=%async_computation | async-start | bytes 13631488 | tf_op jit(solution)/shard_map/all_to_all | solution.py:420
  56.8 11.5 %all-gather.11.cloned.1.call-done = f32[8,520,64]{1,2,0:T(8,128)} async-done(((f32[1,520,64]{1,2,0:T(8,128)}), f32[8,520,64]{1,2,0:T(8,128)}) %all-gather.11.cloned.1.call-update) | async-done | bytes 1064976 | tf_op jit(solution)/shard_map/all_gather | solution.py:430
  69.9 11.7 %cholesky.74 = f32[128,128]{1,0:T(8,128)S(1)} custom-call(f32[128,128]{1,0:T(8,128)S(1)} %copy.225), custom_call_target="Cholesky" | custom-call | tf_op jit(solution)/shard_map/jit(cholesky)/cholesky | solution.py:350
  86.5 11.7 %cholesky.85 = f32[128,128]{1,0:T(8,128)S(1)} custom-call(f32[128,128]{1,0:T(8,128)S(1)} %copy.230), custom_call_target="Cholesky" | custom-call | tf_op jit(solution)/shard_map/jit(cholesky)/cholesky | solution.py:353
  104.3 4.0 add_select_fusion.refs_1_
  114.6 3.2 slot_strips.1
  117.8 30.9 %all-to-all-done.refs_5_ = f32[64,104,256]{2,1,0:T(8,128)} async-done(((f32[64,104,256]{2,1,0:T(8,128)}), f32[64,104,256]{2,1,0:T(8,128)}, u32[]{:S(2)}, u32[]{:S(2)}) %all-to-all-start) | async-done | bytes 6815776 | tf_op jit(solution)/shard_map/all_to_all | solution.py:420
  154.7 14.2 %all-to-all-start.1 = ((f32[64,32,256]{2,1,0:T(8,128)}), f32[64,32,256]{2,1,0:T(8,128)S(1)}, u32[]{:S(2)}, u32[]{:S(2)}) async-start(f32[64,32,256]{2,1,0:T(8,128)} %slot_strips.1), calls=%async_computation.1 | async-start | bytes 4194304 | tf_op jit(solution)/shard_map/all_to_all | solution.py:420
  180.5 5.1 %collective-permute-start.10 = (f32[4,328,64]{1,2,0:T(8,128)S(1)}, f32[4,328,64]{1,2,0:T(8,128)}, u32[]{:S(2)}, u32[]{:S(2)}) collective-permute-start(f32[4,328,64]{1,2,0:T(8,128)S(1)} %pad_maximum_fusion.6), channel_id=1, source_target_pairs={{0,1},{1,0},{2,3},{3,2},{4,5},{5,4},{6,7},{7,6},{8,9},{9,8},{10,11... | collective-permute-start | bytes 1007624 | tf_op jit(solution)/shard_map/ppermute | solution.py:377
  194.4 2.9 slab_strip.1
  199.3 11.7 %cholesky.96 = f32[128,128]{1,0:T(8,128)S(1)} custom-call(f32[128,128]{1,0:T(8,128)S(1)} %copy.251), custom_call_target="Cholesky" | custom-call | tf_op jit(solution)/shard_map/jit(cholesky)/cholesky | solution.py:350
  213.1 6.2 %all-to-all-start.2 = ((f32[64,80,256]{2,1,0:T(8,128)}), f32[64,80,256]{2,1,0:T(8,128)}, u32[]{:S(2)}, u32[]{:S(2)}) async-start(f32[64,80,256]{2,1,0:T(8,128)} %get-tuple-element.68), calls=%async_computation.2 | async-start | bytes 10485760 | tf_op jit(solution)/shard_map/all_to_all | solution.py:420
  222.4 11.7 %cholesky.107 = f32[128,128]{1,0:T(8,128)S(1)} custom-call(f32[128,128]{1,0:T(8,128)S(1)} %fusion.24), custom_call_target="Cholesky" | custom-call | tf_op jit(solution)/shard_map/jit(cholesky)/cholesky | solution.py:353
  239.3 61.4 %all-gather.9.cloned.1.call-done = f32[40,32,512]{2,1,0:T(8,128)} async-done(((f32[10,32,512]{2,1,0:T(8,128)}), f32[40,32,512]{2,1,0:T(8,128)}) %all-gather.9.cloned.1.call-update) | async-done | bytes 2621456 | tf_op jit(solution)/shard_map/all_gather | solution.py:471
  300.7 2.7 fusion.1
  311.1 6.8 %all-to-all-start.3 = ((f32[64,80,256]{2,1,0:T(8,128)}), f32[64,80,256]{2,1,0:T(8,128)}, u32[]{:S(2)}, u32[]{:S(2)}) async-start(f32[64,80,256]{2,1,0:T(8,128)} %get-tuple-element.77), calls=%async_computation.3 | async-start | bytes 10485760 | tf_op jit(solution)/shard_map/all_to_all | solution.py:420
  318.2 2.5 collective-permute-start.13
  320.8 2.5 collective-permute-start.12
  323.4 18.4 %collective-permute-done.11 = f32[2,5,32,512]{3,2,1,0:T(8,128)S(1)} collective-permute-done((f32[2,5,32,512]{3,2,1,0:T(8,128)S(1)}, f32[2,5,32,512]{3,2,1,0:T(8,128)S(1)}, u32[]{:S(2)}, u32[]{:S(2)}) %collective-permute-start.11) | collective-permute-done | bytes 655392 | tf_op jit(solution)/shard_map/ppermute | solution.py:369
  344.9 26.2 %collective-permute-done.12 = f32[2,5,32,512]{3,2,1,0:T(8,128)S(1)} collective-permute-done((f32[2,5,32,512]{3,2,1,0:T(8,128)S(1)}, f32[2,5,32,512]{3,2,1,0:T(8,128)S(1)}, u32[]{:S(2)}, u32[]{:S(2)}) %collective-permute-start.12) | collective-permute-done | bytes 655392 | tf_op jit(solution)/shard_map/ppermute | solution.py:369
  378.5 25.1 %all-to-all-done.3.refs_7_ = f32[64,80,256]{2,1,0:T(8,128)} async-done(((f32[64,80,256]{2,1,0:T(8,128)}), f32[64,80,256]{2,1,0:T(8,128)}, u32[]{:S(2)}, u32[]{:S(2)}) %all-to-all-start.3) | async-done | bytes 5242912 | tf_op jit(solution)/shard_map/all_to_all | solution.py:420
  403.6 19.2 %place_and_update.1 = f32[2560,1280]{1,0:T(8,128)} custom-call(s32[141]{0:T(256)S(1)} %concatenate.68.refs_0_, f32[8,10,32,512]{3,2,1,0:T(8,128)} %all-gather.7.cloned.1.call-done.refs_1_, f32[256,256]{1,0:T(8,128)S(1)} %copy-done, f32[256,256]{1,0:T(8,128)S(1)} %select_maximum_fusion.1.refs_3_, f32[8,5,32,512]{3,2,1,0:T(8,128)S(1)} %bitcast.192, ...), custom_call_target="tpu_custom_call" | custom-call | flops 10066329600 | bytes 26214400 | tf_op jit(solution)/shard_map/place_and_update/pallas_call | solution.py:302
  (234 shorter events, 95.8 us)
Async XLA Ops:
  6.5 61.7 %all-gather.11.cloned.1.call-start = ((), (), s32[]{:S(2)}) async-start(), calls=%async_computation.6 | async-start | bytes 1474560 | tf_op jit(solution)/shard_map/all_gather | solution.py:430
  29.4 10.3 %collective-permute-start.2 = (f32[512,64]{0,1:T(8,128)S(1)}, f32[512,64]{0,1:T(8,128)S(1)}, u32[]{:S(2)}, u32[]{:S(2)}) collective-permute-start(f32[512,64]{0,1:T(8,128)S(1)} %slice_bitcast_fusion.1), channel_id=1, source_target_pairs={{0,24},{1,25},{2,26},{3,27},{4,28},{5,29},{6,30},{7,31},{32,56},{3... | collective-permute-start | bytes 393224 | tf_op jit(solution)/shard_map/ppermute | solution.py:425
  35.1 4.7 %collective-permute-start.1 = (f32[512,64]{0,1:T(8,128)S(1)}, f32[512,64]{0,1:T(8,128)S(1)}, u32[]{:S(2)}, u32[]{:S(2)}) collective-permute-start(f32[512,64]{0,1:T(8,128)S(1)} %slice_bitcast_fusion.1), channel_id=1, source_target_pairs={{0,16},{1,17},{2,18},{3,19},{4,20},{5,21},{6,22},{7,23},{32,48},{3... | collective-permute-start | bytes 393224 | tf_op jit(solution)/shard_map/ppermute | solution.py:425
  36.4 4.9 %collective-permute-start = (f32[512,64]{0,1:T(8,128)S(1)}, f32[512,64]{0,1:T(8,128)S(1)}, u32[]{:S(2)}, u32[]{:S(2)}) collective-permute-start(f32[512,64]{0,1:T(8,128)S(1)} %slice_bitcast_fusion.1), channel_id=1, source_target_pairs={{0,8},{1,9},{2,10},{3,11},{4,12},{5,13},{6,14},{7,15},{32,40},{33,... | collective-permute-start | bytes 393224 | tf_op jit(solution)/shard_map/ppermute | solution.py:425
  42.2 106.5 %all-to-all-start = ((f32[64,104,256]{2,1,0:T(8,128)}), f32[64,104,256]{2,1,0:T(8,128)}, u32[]{:S(2)}, u32[]{:S(2)}) async-start(f32[64,104,256]{2,1,0:T(8,128)} %get-tuple-element.61), calls=%async_computation | async-start | bytes 13631488 | tf_op jit(solution)/shard_map/all_to_all | solution.py:420
  50.6 53.7 %collective-permute-start.3 = (f32[2,32,32,256]{3,2,1,0:T(8,128)}, f32[2,32,32,256]{3,2,1,0:T(8,128)}, u32[]{:S(2)}, u32[]{:S(2)}) collective-permute-start(f32[2,32,32,256]{3,2,1,0:T(8,128)} %get-tuple-element.57), channel_id=1, source_target_pairs={{0,2},{8,10},{16,18},{24,26},{32,34},{40,42},{48,50},{56,58},{64,6... | collective-permute-start | bytes 6291464 | tf_op jit(solution)/shard_map/ppermute | solution.py:433
  52.6 51.7 %collective-permute-start.4 = (f32[2,32,32,256]{3,2,1,0:T(8,128)}, f32[2,32,32,256]{3,2,1,0:T(8,128)}, u32[]{:S(2)}, u32[]{:S(2)}) collective-permute-start(f32[2,32,32,256]{3,2,1,0:T(8,128)} %get-tuple-element.58), channel_id=1, source_target_pairs={{0,4},{8,12},{16,20},{24,28},{32,36},{40,44},{48,52},{56,60},{64,6... | collective-permute-start | bytes 6291464 | tf_op jit(solution)/shard_map/ppermute | solution.py:433
  54.6 49.7 %collective-permute-start.5 = (f32[2,32,32,256]{3,2,1,0:T(8,128)}, f32[2,32,32,256]{3,2,1,0:T(8,128)}, u32[]{:S(2)}, u32[]{:S(2)}) collective-permute-start(f32[2,32,32,256]{3,2,1,0:T(8,128)} %get-tuple-element.59), channel_id=1, source_target_pairs={{0,6},{8,14},{16,22},{24,30},{32,38},{40,46},{48,54},{56,62},{64,7... | collective-permute-start | bytes 6291464 | tf_op jit(solution)/shard_map/ppermute | solution.py:433
  108.5 5.1 %collective-permute-start.6 = (f32[32,32,256]{2,1,0:T(8,128)S(1)}, f32[32,32,256]{2,1,0:T(8,128)S(1)}, u32[]{:S(2)}, u32[]{:S(2)}) collective-permute-start(f32[32,32,256]{2,1,0:T(8,128)S(1)} %slice_bitcast_fusion), channel_id=1, source_target_pairs={{0,1},{2,3},{4,5},{6,7},{8,9},{10,11},{12,13},{14,15},{16,17},{18,... | collective-permute-start | bytes 3145736 | tf_op jit(solution)/shard_map/ppermute | solution.py:435
  151.9 22.8 %collective-permute-start.9 = (f32[2,328,64]{1,2,0:T(8,128)}, f32[2,328,64]{1,2,0:T(8,128)}, u32[]{:S(2)}, u32[]{:S(2)}) collective-permute-start(f32[2,328,64]{1,2,0:T(8,128)} %bitcast.24), channel_id=1, source_target_pairs={{0,6},{1,7},{2,0},{3,1},{4,2},{5,3},{6,4},{7,5},{8,14},{9,15},{10,... | collective-permute-start | bytes 503816 | tf_op jit(solution)/shard_map/ppermute | solution.py:369
  154.7 39.7 %all-to-all-start.1 = ((f32[64,32,256]{2,1,0:T(8,128)}), f32[64,32,256]{2,1,0:T(8,128)S(1)}, u32[]{:S(2)}, u32[]{:S(2)}) async-start(f32[64,32,256]{2,1,0:T(8,128)} %slot_strips.1), calls=%async_computation.1 | async-start | bytes 4194304 | tf_op jit(solution)/shard_map/all_to_all | solution.py:420
  168.9 131.8 %all-gather.9.cloned.1.call-start = ((), (), s32[]{:S(2)}) async-start(), calls=%async_computation.5 | async-start | bytes 3276800 | tf_op jit(solution)/shard_map/all_gather | solution.py:471
  170.8 6.5 %collective-permute-start.8 = (f32[2,328,64]{1,2,0:T(8,128)}, f32[2,328,64]{1,2,0:T(8,128)}, u32[]{:S(2)}, u32[]{:S(2)}) collective-permute-start(f32[2,328,64]{1,2,0:T(8,128)} %bitcast.222), channel_id=1, source_target_pairs={{0,4},{1,5},{2,6},{3,7},{4,0},{5,1},{6,2},{7,3},{8,12},{9,13},{10,... | collective-permute-start | bytes 503816 | tf_op jit(solution)/shard_map/ppermute | solution.py:369
  171.9 14.1 %copy-start.10 = (f32[1,1,328,64]{3,2,1,0:T(8,128)S(1)}, f32[1,1,328,64]{3,2,1,0:T(8,128)}, u32[]{:S(2)}) copy-start(f32[1,1,328,64]{3,2,1,0:T(8,128)} %get-tuple-element.105) | copy-start | bytes 251908
  174.1 6.4 %collective-permute-start.7 = (f32[2,328,64]{1,2,0:T(8,128)S(1)}, f32[2,328,64]{1,2,0:T(8,128)S(1)}, u32[]{:S(2)}, u32[]{:S(2)}) collective-permute-start(f32[2,328,64]{1,2,0:T(8,128)S(1)} %bitcast.223), channel_id=1, source_target_pairs={{0,2},{1,3},{2,4},{3,5},{4,6},{5,7},{6,0},{7,1},{8,10},{9,11},{10,... | collective-permute-start | bytes 503816 | tf_op jit(solution)/shard_map/ppermute | solution.py:369
  180.5 6.6 %collective-permute-start.10 = (f32[4,328,64]{1,2,0:T(8,128)S(1)}, f32[4,328,64]{1,2,0:T(8,128)}, u32[]{:S(2)}, u32[]{:S(2)}) collective-permute-start(f32[4,328,64]{1,2,0:T(8,128)S(1)} %pad_maximum_fusion.6), channel_id=1, source_target_pairs={{0,1},{1,0},{2,3},{3,2},{4,5},{5,4},{6,7},{7,6},{8,9},{9,8},{10,11... | collective-permute-start | bytes 1007624 | tf_op jit(solution)/shard_map/ppermute | solution.py:377
  213.1 87.6 %all-to-all-start.2 = ((f32[64,80,256]{2,1,0:T(8,128)}), f32[64,80,256]{2,1,0:T(8,128)}, u32[]{:S(2)}, u32[]{:S(2)}) async-start(f32[64,80,256]{2,1,0:T(8,128)} %get-tuple-element.68), calls=%async_computation.2 | async-start | bytes 10485760 | tf_op jit(solution)/shard_map/all_to_all | solution.py:420
  219.3 184.3 %all-gather.7.cloned.1.call-start = ((), (), s32[]{:S(2)}) async-start(), calls=%async_computation.4 | async-start | bytes 5898240 | tf_op jit(solution)/shard_map/all_gather | solution.py:488
  311.1 92.6 %all-to-all-start.3 = ((f32[64,80,256]{2,1,0:T(8,128)}), f32[64,80,256]{2,1,0:T(8,128)}, u32[]{:S(2)}, u32[]{:S(2)}) async-start(f32[64,80,256]{2,1,0:T(8,128)} %get-tuple-element.77), calls=%async_computation.3 | async-start | bytes 10485760 | tf_op jit(solution)/shard_map/all_to_all | solution.py:420
  318.0 23.7 %collective-permute-start.11 = (f32[2,5,32,512]{3,2,1,0:T(8,128)S(1)}, f32[2,5,32,512]{3,2,1,0:T(8,128)S(1)}, u32[]{:S(2)}, u32[]{:S(2)}) collective-permute-start(f32[2,5,32,512]{3,2,1,0:T(8,128)S(1)} %get-tuple-element.102), channel_id=1, source_target_pairs={{0,2},{1,3},{2,4},{3,5},{4,6},{5,7},{6,0},{7,1},{8,10},{9,11},{10,... | collective-permute-start | bytes 1966088 | tf_op jit(solution)/shard_map/ppermute | solution.py:369
  318.2 25.9 %collective-permute-start.13 = (f32[2,5,32,512]{3,2,1,0:T(8,128)S(1)}, f32[2,5,32,512]{3,2,1,0:T(8,128)S(1)}, u32[]{:S(2)}, u32[]{:S(2)}) collective-permute-start(f32[2,5,32,512]{3,2,1,0:T(8,128)S(1)} %get-tuple-element.103), channel_id=1, source_target_pairs={{0,6},{1,7},{2,0},{3,1},{4,2},{5,3},{6,4},{7,5},{8,14},{9,15},{10,... | collective-permute-start | bytes 1966088 | tf_op jit(solution)/shard_map/ppermute | solution.py:369
  320.8 50.4 %collective-permute-start.12 = (f32[2,5,32,512]{3,2,1,0:T(8,128)S(1)}, f32[2,5,32,512]{3,2,1,0:T(8,128)S(1)}, u32[]{:S(2)}, u32[]{:S(2)}) collective-permute-start(f32[2,5,32,512]{3,2,1,0:T(8,128)S(1)} %get-tuple-element.104), channel_id=1, source_target_pairs={{0,4},{1,5},{2,6},{3,7},{4,0},{5,1},{6,2},{7,3},{8,12},{9,13},{10,... | collective-permute-start | bytes 1966088 | tf_op jit(solution)/shard_map/ppermute | solution.py:369
  372.1 4.3 collective-permute-start.14
  378.2 25.4 %copy-start = (f32[256,256]{1,0:T(8,128)S(1)}, f32[256,256]{1,0:T(8,128)}, u32[]{:S(2)}) copy-start(f32[256,256]{1,0:T(8,128)} %select_maximum_fusion.3.refs_2_) | copy-start | bytes 786436
  (11 other events, 29.7 us)
Sparse Core Ops, SparseCore 0:
  42.3 25.9 all-gather.10
  213.2 87.4 all-gather.8
  311.2 59.1 all-gather.6

commit v2 on v0

--- a/solution.py
+++ b/solution.py
@@ -13,7 +13,7 @@
 NSTRIP = BS // STRIP
 NCHIP = NSTRIP // 2
 MARK = 8
-PARTS = (64, 96, 96)
+PARTS = (96, 88, 72)
 OFFSETS = tuple(sum(PARTS[:q]) for q in range(len(PARTS)))
 NPART = len(PARTS)
 GROUP = 8

time: 448 us -> 410 us (0.915)
  the two profiles are of different devices: /device:TPU:124 before, /device:TPU:7 now
where the time goes in v2:
time: 410 us; the launch traced here: 403 us
  waiting for transfers between devices  167 us (41%)
  other arithmetic  76.3 us (19%)
  starting transfers between devices  63.5 us (15%)
  Pallas kernels  45.3 us (11%)
  local copies, waits for them, and re-layouts  20.4 us (5%)
  matrix products  15.7 us (4%)
  between operations  15.5 us (4%)
    all_gather x1, waiting for transfers between devices, body(): rows = lax.all_gather(solved, 'row', axis=0)  86.3 us
    ppermute x6, waiting for transfers between devices, exchange(): lax.ppermute(pair, 'col', [(c, (c + 2 * step) % n_col) for c in range(n_c...  52.4 us
    all_to_all x4, starting transfers between devices, send(): lax.all_to_all(part, ('front', 'row'), split_axis=0, concat_axis=0, tiled...  33.7 us
    another operation x6, other arithmetic, panel(): jnp.linalg.cholesky(lower_sym(block[half:, half:] - dot(below, below.T)))  24.8 us
    another operation x6, other arithmetic, panel(): first = jnp.linalg.cholesky(lower_sym(block[:half, :half]))  24.8 us
    pallas_call x1, Pallas kernels, final(): pl.pallas_call(lambda *refs: final_kernel(col_blocks, *refs), grid_spec=p...  22.4 us
    all_to_all x4, waiting for transfers between devices, send(): lax.all_to_all(part, ('front', 'row'), split_axis=0, concat_axis=0, tiled...  17.4 us
    pallas_call x1, Pallas kernels, permute(): pl.pallas_call(permute_kernel, grid_spec=pltpu.PrefetchScalarGridSpec(num...  16.9 us
  transfers between devices with their start and end apart: 22, of which 12 were waited for; matrix products, arithmetic and copies ran while one was open for 26% of the time, Pallas kernels for 5%

profile of v2, /device:TPU:7, one launch (start us, length us, event | category | flops | bytes accessed | tf_op | source)
XLA Modules:
  0.0 403.4 jit_solution(6646237979191181758)
XLA Ops:
  7.5 5.7 %collective-permute-start.2 = (f32[512,64]{0,1:T(8,128)S(1)}, f32[512,64]{0,1:T(8,128)S(1)}, u32[]{:S(2)}, u32[]{:S(2)}) collective-permute-start(f32[512,64]{0,1:T(8,128)S(1)} %slice_bitcast_fusion.1), channel_id=1, source_target_pairs={{0,24},{1,25},{2,26},{3,27},{4,28},{5,29},{6,30},{7,31},{32,56},{3... | collective-permute-start | bytes 393224 | tf_op jit(solution)/shard_map/ppermute | solution.py:420
  26.5 16.9 %permute_tiles.1 = (f32[2,32,32,256]{3,2,1,0:T(8,128)}, f32[2,32,32,256]{3,2,1,0:T(8,128)}, f32[2,32,32,256]{3,2,1,0:T(8,128)}, f32[2,32,32,256]{3,2,1,0:T(8,128...) custom-call(s32[32]{0:T(128)} %copy-done.13, s32[64]{0:T(128)} %broadcast_select_fusion.1.label_ref, ...), custom_call_target="tpu_custom_call" | custom-call | flops 6442450944 | bytes 25165824 | tf_op jit(solution)/shard_map/permute_tiles/pallas_call | solution.py:97
  43.4 6.2 %all-to-all-start = ((f32[64,104,256]{2,1,0:T(8,128)}), f32[64,104,256]{2,1,0:T(8,128)}, u32[]{:S(2)}, u32[]{:S(2)}) async-start(f32[64,104,256]{2,1,0:T(8,128)} %get-tuple-element.48), calls=%async_computation | async-start | bytes 13631488 | tf_op jit(solution)/shard_map/all_to_all | solution.py:430
  57.4 11.7 %cholesky.74 = f32[128,128]{1,0:T(8,128)S(1)} custom-call(f32[128,128]{1,0:T(8,128)S(1)} %copy.211), custom_call_target="Cholesky" | custom-call | tf_op jit(solution)/shard_map/jit(cholesky)/cholesky | solution.py:350
  73.8 11.7 %cholesky.85 = f32[128,128]{1,0:T(8,128)S(1)} custom-call(f32[128,128]{1,0:T(8,128)S(1)} %copy.216), custom_call_target="Cholesky" | custom-call | tf_op jit(solution)/shard_map/jit(cholesky)/cholesky | solution.py:353
  91.4 11.7 %cholesky.96 = f32[128,128]{1,0:T(8,128)S(1)} custom-call(f32[128,128]{1,0:T(8,128)S(1)} %copy.228), custom_call_target="Cholesky" | custom-call | tf_op jit(solution)/shard_map/jit(cholesky)/cholesky | solution.py:350
  108.0 11.7 %cholesky.107 = f32[128,128]{1,0:T(8,128)S(1)} custom-call(f32[128,128]{1,0:T(8,128)S(1)} %fusion.25), custom_call_target="Cholesky" | custom-call | tf_op jit(solution)/shard_map/jit(cholesky)/cholesky | solution.py:353
  126.6 4.1 %add_select_fusion.refs_1_ = f32[2,32,32,256]{3,2,1,0:T(8,128)S(1)} fusion(f32[2,32,32,256]{3,2,1,0:T(8,128)S(1)} %copy-done.4, f32[2,32,32,256]{3,2,1,0:T(8,128)} %collective-permute-done.5, f32[2,32,32,256]{3,2,1,0:T(8,128)} %collective-permute-done.3, f32[2,32,32,256]{3,2,1,0:T(8,128)} %collective-permute-done.4, pred[]{:T(512)S(6)} %eq.153), kind=kLoop, calls=%fused_computation.14 | loop fusion | flops 1572864 | bytes 10485761 | tf_op jit(solution)/shard_map/jit(_where)/select_n | solution.py:435
  135.4 6.1 %collective-permute-done.6.refs_2_ = f32[32,32,256]{2,1,0:T(8,128)} collective-permute-done((f32[32,32,256]{2,1,0:T(8,128)S(1)}, f32[32,32,256]{2,1,0:T(8,128)}, u32[]{:S(2)}, u32[]{:S(2)}) %collective-permute-start.6) | collective-permute-done | bytes 1048608 | tf_op jit(solution)/shard_map/ppermute | solution.py:436
  141.5 3.2 slot_strips.1
  144.7 4.7 %all-to-all-done.refs_5_ = f32[64,104,256]{2,1,0:T(8,128)} async-done(((f32[64,104,256]{2,1,0:T(8,128)}), f32[64,104,256]{2,1,0:T(8,128)}, u32[]{:S(2)}, u32[]{:S(2)}) %all-to-all-start) | async-done | bytes 6815776 | tf_op jit(solution)/shard_map/all_to_all | solution.py:430
  155.0 14.5 %all-to-all-start.1 = ((f32[64,32,256]{2,1,0:T(8,128)}), f32[64,32,256]{2,1,0:T(8,128)S(1)}, u32[]{:S(2)}, u32[]{:S(2)}) async-start(f32[64,32,256]{2,1,0:T(8,128)} %slot_strips.1), calls=%async_computation.1 | async-start | bytes 4194304 | tf_op jit(solution)/shard_map/all_to_all | solution.py:430
  178.8 4.2 %collective-permute-done.7 = f32[2,328,64]{1,2,0:T(8,128)S(1)} collective-permute-done((f32[2,328,64]{1,2,0:T(8,128)S(1)}, f32[2,328,64]{1,2,0:T(8,128)S(1)}, u32[]{:S(2)}, u32[]{:S(2)}) %collective-permute-start.7) | collective-permute-done | bytes 167968 | tf_op jit(solution)/shard_map/ppermute | solution.py:369
  183.0 3.3 collective-permute-start.10
  195.2 2.8 slab_strip.1
  200.3 5.9 %all-to-all-start.2 = ((f32[64,88,256]{2,1,0:T(8,128)}), f32[64,88,256]{2,1,0:T(8,128)}, u32[]{:S(2)}, u32[]{:S(2)}) async-start(f32[64,88,256]{2,1,0:T(8,128)} %get-tuple-element.57), calls=%async_computation.2 | async-start | bytes 11534336 | tf_op jit(solution)/shard_map/all_to_all | solution.py:430
  207.0 86.3 %all-gather.8.cloned.1.call-done = f32[40,32,512]{2,1,0:T(8,128)} async-done(((f32[10,32,512]{2,1,0:T(8,128)}), f32[40,32,512]{2,1,0:T(8,128)}) %all-gather.8.cloned.1.call-update) | async-done | bytes 2621456 | tf_op jit(solution)/shard_map/all_gather | solution.py:486
  293.3 7.2 %all-to-all-start.3 = ((f32[64,72,256]{2,1,0:T(8,128)}), f32[64,72,256]{2,1,0:T(8,128)}, u32[]{:S(2)}, u32[]{:S(2)}) async-start(f32[64,72,256]{2,1,0:T(8,128)} %get-tuple-element.63), calls=%async_computation.3 | async-start | bytes 9437184 | tf_op jit(solution)/shard_map/all_to_all | solution.py:430
  303.4 2.7 collective-permute-start.12
  306.2 16.7 %collective-permute-done.11 = f32[2,5,32,512]{3,2,1,0:T(8,128)S(1)} collective-permute-done((f32[2,5,32,512]{3,2,1,0:T(8,128)S(1)}, f32[2,5,32,512]{3,2,1,0:T(8,128)S(1)}, u32[]{:S(2)}, u32[]{:S(2)}) %collective-permute-start.11) | collective-permute-done | bytes 655392 | tf_op jit(solution)/shard_map/ppermute | solution.py:369
  322.9 2.7 collective-permute-done.13
  326.3 27.5 %collective-permute-done.12 = f32[2,5,32,512]{3,2,1,0:T(8,128)S(1)} collective-permute-done((f32[2,5,32,512]{3,2,1,0:T(8,128)S(1)}, f32[2,5,32,512]{3,2,1,0:T(8,128)S(1)}, u32[]{:S(2)}, u32[]{:S(2)}) %collective-permute-start.12) | collective-permute-done | bytes 655392 | tf_op jit(solution)/shard_map/ppermute | solution.py:369
  361.3 12.8 %all-to-all-done.3.refs_7_ = f32[64,72,256]{2,1,0:T(8,128)} async-done(((f32[64,72,256]{2,1,0:T(8,128)}), f32[64,72,256]{2,1,0:T(8,128)}, u32[]{:S(2)}, u32[]{:S(2)}) %all-to-all-start.3) | async-done | bytes 4718624 | tf_op jit(solution)/shard_map/all_to_all | solution.py:430
  374.1 22.4 %place_and_update.1 = f32[2560,1280]{1,0:T(8,128)} custom-call(s32[141]{0:T(256)S(1)} %concatenate.74.refs_0_, f32[8,10,32,512]{3,2,1,0:T(8,128)} %bitcast.205, f32[256,256]{1,0:T(8,128)S(1)} %copy-done, f32[256,256]{1,0:T(8,128)S(1)} %copy-done.1, f32[8,5,32,512]{3,2,1,0:T(8,128)S(1)} %bitcast.196, f32[64,104,256]{2,1,0:T(8,128)} %all-to-all-done.refs_5_, ...), custom_call_target="tpu_custom_call" | custom-call | flops 10066329600 | bytes 26214400 | tf_op jit(solution)/shard_map/place_and_update/pallas_call | solution.py:302
  (239 shorter events, 85.6 us)
Async XLA Ops:
  6.5 17.1 %copy-start.9 = (s32[32,256]{1,0:T(8,128)S(1)}, s32[32,256]{1,0:T(8,128)}, u32[]{:S(2)}) copy-start(s32[32,256]{1,0:T(8,128)} %param.15) | copy-start | bytes 98308
  6.5 17.7 %copy-start.10 = (s32[32,256]{1,0:T(8,128)S(1)}, s32[32,256]{1,0:T(8,128)}, u32[]{:S(2)}) copy-start(s32[32,256]{1,0:T(8,128)} %param.16) | copy-start | bytes 98308
  6.5 49.2 %all-gather.12.cloned.1.call-start = ((), (), s32[]{:S(2)}) async-start(), calls=%async_computation.6 | async-start | bytes 1474560 | tf_op jit(solution)/shard_map/all_gather | solution.py:425
  7.5 11.2 %collective-permute-start.2 = (f32[512,64]{0,1:T(8,128)S(1)}, f32[512,64]{0,1:T(8,128)S(1)}, u32[]{:S(2)}, u32[]{:S(2)}) collective-permute-start(f32[512,64]{0,1:T(8,128)S(1)} %slice_bitcast_fusion.1), channel_id=1, source_target_pairs={{0,24},{1,25},{2,26},{3,27},{4,28},{5,29},{6,30},{7,31},{32,56},{3... | collective-permute-start | bytes 393224 | tf_op jit(solution)/shard_map/ppermute | solution.py:420
  13.2 5.5 %collective-permute-start.1 = (f32[512,64]{0,1:T(8,128)S(1)}, f32[512,64]{0,1:T(8,128)S(1)}, u32[]{:S(2)}, u32[]{:S(2)}) collective-permute-start(f32[512,64]{0,1:T(8,128)S(1)} %slice_bitcast_fusion.1), channel_id=1, source_target_pairs={{0,16},{1,17},{2,18},{3,19},{4,20},{5,21},{6,22},{7,23},{32,48},{3... | collective-permute-start | bytes 393224 | tf_op jit(solution)/shard_map/ppermute | solution.py:420
  14.5 4.9 %collective-permute-start = (f32[512,64]{0,1:T(8,128)S(1)}, f32[512,64]{0,1:T(8,128)S(1)}, u32[]{:S(2)}, u32[]{:S(2)}) collective-permute-start(f32[512,64]{0,1:T(8,128)S(1)} %slice_bitcast_fusion.1), channel_id=1, source_target_pairs={{0,8},{1,9},{2,10},{3,11},{4,12},{5,13},{6,14},{7,15},{32,40},{33,... | collective-permute-start | bytes 393224 | tf_op jit(solution)/shard_map/ppermute | solution.py:420
  43.4 105.9 %all-to-all-start = ((f32[64,104,256]{2,1,0:T(8,128)}), f32[64,104,256]{2,1,0:T(8,128)}, u32[]{:S(2)}, u32[]{:S(2)}) async-start(f32[64,104,256]{2,1,0:T(8,128)} %get-tuple-element.48), calls=%async_computation | async-start | bytes 13631488 | tf_op jit(solution)/shard_map/all_to_all | solution.py:430
  49.6 77.0 %collective-permute-start.3 = (f32[2,32,32,256]{3,2,1,0:T(8,128)}, f32[2,32,32,256]{3,2,1,0:T(8,128)}, u32[]{:S(2)}, u32[]{:S(2)}) collective-permute-start(f32[2,32,32,256]{3,2,1,0:T(8,128)} %get-tuple-element.44), channel_id=1, source_target_pairs={{0,2},{8,10},{16,18},{24,26},{32,34},{40,42},{48,50},{56,58},{64,6... | collective-permute-start | bytes 6291464 | tf_op jit(solution)/shard_map/ppermute | solution.py:434
  51.6 75.0 %collective-permute-start.4 = (f32[2,32,32,256]{3,2,1,0:T(8,128)}, f32[2,32,32,256]{3,2,1,0:T(8,128)}, u32[]{:S(2)}, u32[]{:S(2)}) collective-permute-start(f32[2,32,32,256]{3,2,1,0:T(8,128)} %get-tuple-element.45), channel_id=1, source_target_pairs={{0,4},{8,12},{16,20},{24,28},{32,36},{40,44},{48,52},{56,60},{64,6... | collective-permute-start | bytes 6291464 | tf_op jit(solution)/shard_map/ppermute | solution.py:434
  53.6 73.0 %collective-permute-start.5 = (f32[2,32,32,256]{3,2,1,0:T(8,128)}, f32[2,32,32,256]{3,2,1,0:T(8,128)}, u32[]{:S(2)}, u32[]{:S(2)}) collective-permute-start(f32[2,32,32,256]{3,2,1,0:T(8,128)} %get-tuple-element.46), channel_id=1, source_target_pairs={{0,6},{8,14},{16,22},{24,30},{32,38},{40,46},{48,54},{56,62},{64,7... | collective-permute-start | bytes 6291464 | tf_op jit(solution)/shard_map/ppermute | solution.py:434
  130.8 10.7 %collective-permute-start.6 = (f32[32,32,256]{2,1,0:T(8,128)S(1)}, f32[32,32,256]{2,1,0:T(8,128)}, u32[]{:S(2)}, u32[]{:S(2)}) collective-permute-start(f32[32,32,256]{2,1,0:T(8,128)S(1)} %slice_bitcast_fusion), channel_id=1, source_target_pairs={{0,1},{2,3},{4,5},{6,7},{8,9},{10,11},{12,13},{14,15},{16,17},{18,... | collective-permute-start | bytes 3145736 | tf_op jit(solution)/shard_map/ppermute | solution.py:436
  152.6 22.9 %collective-permute-start.9 = (f32[2,328,64]{1,2,0:T(8,128)}, f32[2,328,64]{1,2,0:T(8,128)}, u32[]{:S(2)}, u32[]{:S(2)}) collective-permute-start(f32[2,328,64]{1,2,0:T(8,128)} %bitcast.30), channel_id=1, source_target_pairs={{0,6},{1,7},{2,0},{3,1},{4,2},{5,3},{6,4},{7,5},{8,14},{9,15},{10,... | collective-permute-start | bytes 503816 | tf_op jit(solution)/shard_map/ppermute | solution.py:369
  155.0 40.1 %all-to-all-start.1 = ((f32[64,32,256]{2,1,0:T(8,128)}), f32[64,32,256]{2,1,0:T(8,128)S(1)}, u32[]{:S(2)}, u32[]{:S(2)}) async-start(f32[64,32,256]{2,1,0:T(8,128)} %slot_strips.1), calls=%async_computation.1 | async-start | bytes 4194304 | tf_op jit(solution)/shard_map/all_to_all | solution.py:430
  171.3 6.5 %collective-permute-start.8 = (f32[2,328,64]{1,2,0:T(8,128)}, f32[2,328,64]{1,2,0:T(8,128)}, u32[]{:S(2)}, u32[]{:S(2)}) collective-permute-start(f32[2,328,64]{1,2,0:T(8,128)} %bitcast.228), channel_id=1, source_target_pairs={{0,4},{1,5},{2,6},{3,7},{4,0},{5,1},{6,2},{7,3},{8,12},{9,13},{10,... | collective-permute-start | bytes 503816 | tf_op jit(solution)/shard_map/ppermute | solution.py:369
  174.8 8.2 %collective-permute-start.7 = (f32[2,328,64]{1,2,0:T(8,128)S(1)}, f32[2,328,64]{1,2,0:T(8,128)S(1)}, u32[]{:S(2)}, u32[]{:S(2)}) collective-permute-start(f32[2,328,64]{1,2,0:T(8,128)S(1)} %bitcast.229), channel_id=1, source_target_pairs={{0,2},{1,3},{2,4},{3,5},{4,6},{5,7},{6,0},{7,1},{8,10},{9,11},{10,... | collective-permute-start | bytes 503816 | tf_op jit(solution)/shard_map/ppermute | solution.py:369
  183.0 4.8 %collective-permute-start.10 = (f32[4,328,64]{1,2,0:T(8,128)S(1)}, f32[4,328,64]{1,2,0:T(8,128)}, u32[]{:S(2)}, u32[]{:S(2)}) collective-permute-start(f32[4,328,64]{1,2,0:T(8,128)S(1)} %pad_maximum_fusion.6), channel_id=1, source_target_pairs={{0,1},{1,0},{2,3},{3,2},{4,5},{5,4},{6,7},{7,6},{8,9},{9,8},{10,11... | collective-permute-start | bytes 1007624 | tf_op jit(solution)/shard_map/ppermute | solution.py:377
  200.3 92.9 %all-to-all-start.2 = ((f32[64,88,256]{2,1,0:T(8,128)}), f32[64,88,256]{2,1,0:T(8,128)}, u32[]{:S(2)}, u32[]{:S(2)}) async-start(f32[64,88,256]{2,1,0:T(8,128)} %get-tuple-element.57), calls=%async_computation.2 | async-start | bytes 11534336 | tf_op jit(solution)/shard_map/all_to_all | solution.py:430
  206.2 87.0 %all-gather.8.cloned.1.call-start = ((), (), s32[]{:S(2)}) async-start(), calls=%async_computation.4 | async-start | bytes 3276800 | tf_op jit(solution)/shard_map/all_gather | solution.py:486
  206.9 167.1 %all-gather.10.cloned.1.call-start = ((), (), s32[]{:S(2)}) async-start(), calls=%async_computation.5 | async-start | bytes 5898240 | tf_op jit(solution)/shard_map/all_gather | solution.py:490
  293.3 80.8 %all-to-all-start.3 = ((f32[64,72,256]{2,1,0:T(8,128)}), f32[64,72,256]{2,1,0:T(8,128)}, u32[]{:S(2)}, u32[]{:S(2)}) async-start(f32[64,72,256]{2,1,0:T(8,128)} %get-tuple-element.63), calls=%async_computation.3 | async-start | bytes 9437184 | tf_op jit(solution)/shard_map/all_to_all | solution.py:430
  300.7 22.2 %collective-permute-start.11 = (f32[2,5,32,512]{3,2,1,0:T(8,128)S(1)}, f32[2,5,32,512]{3,2,1,0:T(8,128)S(1)}, u32[]{:S(2)}, u32[]{:S(2)}) collective-permute-start(f32[2,5,32,512]{3,2,1,0:T(8,128)S(1)} %get-tuple-element.90), channel_id=1, source_target_pairs={{0,2},{1,3},{2,4},{3,5},{4,6},{5,7},{6,0},{7,1},{8,10},{9,11},{10,... | collective-permute-start | bytes 1966088 | tf_op jit(solution)/shard_map/ppermute | solution.py:369
  302.3 23.3 %collective-permute-start.13 = (f32[2,5,32,512]{3,2,1,0:T(8,128)S(1)}, f32[2,5,32,512]{3,2,1,0:T(8,128)S(1)}, u32[]{:S(2)}, u32[]{:S(2)}) collective-permute-start(f32[2,5,32,512]{3,2,1,0:T(8,128)S(1)} %get-tuple-element.91), channel_id=1, source_target_pairs={{0,6},{1,7},{2,0},{3,1},{4,2},{5,3},{6,4},{7,5},{8,14},{9,15},{10,... | collective-permute-start | bytes 1966088 | tf_op jit(solution)/shard_map/ppermute | solution.py:369
  303.4 50.4 %collective-permute-start.12 = (f32[2,5,32,512]{3,2,1,0:T(8,128)S(1)}, f32[2,5,32,512]{3,2,1,0:T(8,128)S(1)}, u32[]{:S(2)}, u32[]{:S(2)}) collective-permute-start(f32[2,5,32,512]{3,2,1,0:T(8,128)S(1)} %get-tuple-element.92), channel_id=1, source_target_pairs={{0,4},{1,5},{2,6},{3,7},{4,0},{5,1},{6,2},{7,3},{8,12},{9,13},{10,... | collective-permute-start | bytes 1966088 | tf_op jit(solution)/shard_map/ppermute | solution.py:369
  354.7 4.4 %collective-permute-start.14 = (f32[4,5,32,512]{3,2,1,0:T(8,128)S(1)}, f32[4,5,32,512]{3,2,1,0:T(8,128)S(1)}, u32[]{:S(2)}, u32[]{:S(2)}) collective-permute-start(f32[4,5,32,512]{3,2,1,0:T(8,128)S(1)} %pad_maximum_fusion.2), channel_id=1, source_target_pairs={{0,1},{1,0},{2,3},{3,2},{4,5},{5,4},{6,7},{7,6},{8,9},{9,8},{10,11... | collective-permute-start | bytes 3932168 | tf_op jit(solution)/shard_map/ppermute | solution.py:377
  (14 other events, 112.4 us)
Sparse Core Ops, SparseCore 0:
  21.3 26.1 all-gather.11
  208.7 84.5 all-gather.7
  294.9 59.5 all-gather.9

commit v3 on v2

--- a/solution.py
+++ b/solution.py
@@ -79,7 +79,7 @@
             ).start()
         return carry
 
-    lax.fori_loop(0, GROUP, move, 0, unroll=2)
+    lax.fori_loop(0, GROUP, move, 0, unroll=4)
 
     @pl.when(step == pl.num_programs(0) - 1)
     def _():

time: 410 us -> 414 us (level)
  starting transfers between devices: 63.5 us -> 75.1 us
  Pallas kernels: 45.3 us -> 38.1 us
    all_to_all x4, starting transfers between devices: 33.7 us -> 42.8 us  [send(): lax.all_to_all(part, ('front', 'row'), split_axis=0, concat_axis=0, tiled...]
  transfers between devices with their start and end apart: 22 -> 22, of which waited for: 12 -> 12; matrix products, arithmetic and copies ran while one was open for 26% -> 26% of each run, Pallas kernels for 5% -> 4%
where the time goes in v3:
time: 414 us; the launch traced here: 406 us
  waiting for transfers between devices  165 us (40%)
  other arithmetic  76.3 us (18%)
  starting transfers between devices  75.1 us (18%)
  Pallas kernels  38.1 us (9%)
  local copies, waits for them, and re-layouts  20.4 us (5%)
  matrix products  15.7 us (4%)
  between operations  15.3 us (4%)
    all_gather x1, waiting for transfers between devices, body(): rows = lax.all_gather(solved, 'row', axis=0)  86.3 us
    ppermute x6, waiting for transfers between devices, exchange(): lax.ppermute(pair, 'col', [(c, (c + 2 * step) % n_col) for c in range(n_c...  50.3 us
    all_to_all x4, starting transfers between devices, send(): lax.all_to_all(part, ('front', 'row'), split_axis=0, concat_axis=0, tiled...  42.8 us
    another operation x6, other arithmetic, panel(): jnp.linalg.cholesky(lower_sym(block[half:, half:] - dot(below, below.T)))  24.8 us
    another operation x6, other arithmetic, panel(): first = jnp.linalg.cholesky(lower_sym(block[:half, :half]))  24.8 us
    pallas_call x1, Pallas kernels, final(): pl.pallas_call(lambda *refs: final_kernel(col_blocks, *refs), grid_spec=p...  19.3 us
    all_to_all x4, waiting for transfers between devices, send(): lax.all_to_all(part, ('front', 'row'), split_axis=0, concat_axis=0, tiled...  17.7 us
    dot_general x62, matrix products, dot(): return jnp.dot(a, b, precision=HIGH)  15.7 us
  transfers between devices with their start and end apart: 22, of which 12 were waited for; matrix products, arithmetic and copies ran while one was open for 26% of the time, Pallas kernels for 4%

profile of v3, /device:TPU:7, one launch (start us, length us, event | category | flops | bytes accessed | tf_op | source)
XLA Modules:
  0.0 405.7 jit_solution(16375235216998871550)
XLA Ops:
  7.5 5.7 %collective-permute-start.2 = (f32[512,64]{0,1:T(8,128)S(1)}, f32[512,64]{0,1:T(8,128)S(1)}, u32[]{:S(2)}, u32[]{:S(2)}) collective-permute-start(f32[512,64]{0,1:T(8,128)S(1)} %slice_bitcast_fusion.1), channel_id=1, source_target_pairs={{0,24},{1,25},{2,26},{3,27},{4,28},{5,29},{6,30},{7,31},{32,56},{3... | collective-permute-start | bytes 393224 | tf_op jit(solution)/shard_map/ppermute | solution.py:420
  26.5 13.8 %permute_tiles.1 = (f32[2,32,32,256]{3,2,1,0:T(8,128)}, f32[2,32,32,256]{3,2,1,0:T(8,128)}, f32[2,32,32,256]{3,2,1,0:T(8,128)}, f32[2,32,32,256]{3,2,1,0:T(8,128...) custom-call(s32[32]{0:T(128)} %copy-done.13, s32[64]{0:T(128)} %broadcast_select_fusion.1.label_ref, ...), custom_call_target="tpu_custom_call" | custom-call | flops 6442450944 | bytes 25165824 | tf_op jit(solution)/shard_map/permute_tiles/pallas_call | solution.py:97
  40.3 6.3 %all-to-all-start = ((f32[64,104,256]{2,1,0:T(8,128)}), f32[64,104,256]{2,1,0:T(8,128)}, u32[]{:S(2)}, u32[]{:S(2)}) async-start(f32[64,104,256]{2,1,0:T(8,128)} %get-tuple-element.48), calls=%async_computation | async-start | bytes 13631488 | tf_op jit(solution)/shard_map/all_to_all | solution.py:430
  50.6 2.4 collective-permute-start.5
  54.7 11.7 %cholesky.74 = f32[128,128]{1,0:T(8,128)S(1)} custom-call(f32[128,128]{1,0:T(8,128)S(1)} %copy.211), custom_call_target="Cholesky" | custom-call | tf_op jit(solution)/shard_map/jit(cholesky)/cholesky | solution.py:350
  71.1 11.7 %cholesky.85 = f32[128,128]{1,0:T(8,128)S(1)} custom-call(f32[128,128]{1,0:T(8,128)S(1)} %copy.216), custom_call_target="Cholesky" | custom-call | tf_op jit(solution)/shard_map/jit(cholesky)/cholesky | solution.py:353
  88.7 11.7 %cholesky.96 = f32[128,128]{1,0:T(8,128)S(1)} custom-call(f32[128,128]{1,0:T(8,128)S(1)} %copy.228), custom_call_target="Cholesky" | custom-call | tf_op jit(solution)/shard_map/jit(cholesky)/cholesky | solution.py:350
  105.3 11.7 %cholesky.107 = f32[128,128]{1,0:T(8,128)S(1)} custom-call(f32[128,128]{1,0:T(8,128)S(1)} %fusion.25), custom_call_target="Cholesky" | custom-call | tf_op jit(solution)/shard_map/jit(cholesky)/cholesky | solution.py:353
  123.9 4.0 add_select_fusion.refs_1_
  132.6 6.0 %collective-permute-done.6.refs_2_ = f32[32,32,256]{2,1,0:T(8,128)} collective-permute-done((f32[32,32,256]{2,1,0:T(8,128)S(1)}, f32[32,32,256]{2,1,0:T(8,128)}, u32[]{:S(2)}, u32[]{:S(2)}) %collective-permute-start.6) | collective-permute-done | bytes 1048608 | tf_op jit(solution)/shard_map/ppermute | solution.py:436
  138.6 3.2 slot_strips.1
  141.8 7.1 %all-to-all-done.refs_5_ = f32[64,104,256]{2,1,0:T(8,128)} async-done(((f32[64,104,256]{2,1,0:T(8,128)}), f32[64,104,256]{2,1,0:T(8,128)}, u32[]{:S(2)}, u32[]{:S(2)}) %all-to-all-start) | async-done | bytes 6815776 | tf_op jit(solution)/shard_map/all_to_all | solution.py:430
  152.4 14.2 %all-to-all-start.1 = ((f32[64,32,256]{2,1,0:T(8,128)}), f32[64,32,256]{2,1,0:T(8,128)S(1)}, u32[]{:S(2)}, u32[]{:S(2)}) async-start(f32[64,32,256]{2,1,0:T(8,128)} %slot_strips.1), calls=%async_computation.1 | async-start | bytes 4194304 | tf_op jit(solution)/shard_map/all_to_all | solution.py:430
  177.5 6.1 %collective-permute-start.10 = (f32[4,328,64]{1,2,0:T(8,128)S(1)}, f32[4,328,64]{1,2,0:T(8,128)}, u32[]{:S(2)}, u32[]{:S(2)}) collective-permute-start(f32[4,328,64]{1,2,0:T(8,128)S(1)} %pad_maximum_fusion.6), channel_id=1, source_target_pairs={{0,1},{1,0},{2,3},{3,2},{4,5},{5,4},{6,7},{7,6},{8,9},{9,8},{10,11... | collective-permute-start | bytes 1007624 | tf_op jit(solution)/shard_map/ppermute | solution.py:377
  196.5 7.2 %all-to-all-start.2 = ((f32[64,88,256]{2,1,0:T(8,128)}), f32[64,88,256]{2,1,0:T(8,128)}, u32[]{:S(2)}, u32[]{:S(2)}) async-start(f32[64,88,256]{2,1,0:T(8,128)} %get-tuple-element.57), calls=%async_computation.2 | async-start | bytes 11534336 | tf_op jit(solution)/shard_map/all_to_all | solution.py:430
  204.5 86.3 %all-gather.8.cloned.1.call-done = f32[40,32,512]{2,1,0:T(8,128)} async-done(((f32[10,32,512]{2,1,0:T(8,128)}), f32[40,32,512]{2,1,0:T(8,128)}) %all-gather.8.cloned.1.call-update) | async-done | bytes 2621456 | tf_op jit(solution)/shard_map/all_gather | solution.py:486
  290.8 15.2 %all-to-all-start.3 = ((f32[64,72,256]{2,1,0:T(8,128)}), f32[64,72,256]{2,1,0:T(8,128)}, u32[]{:S(2)}, u32[]{:S(2)}) async-start(f32[64,72,256]{2,1,0:T(8,128)} %get-tuple-element.63), calls=%async_computation.3 | async-start | bytes 9437184 | tf_op jit(solution)/shard_map/all_to_all | solution.py:430
  306.2 4.5 %collective-permute-start.11 = (f32[2,5,32,512]{3,2,1,0:T(8,128)S(1)}, f32[2,5,32,512]{3,2,1,0:T(8,128)S(1)}, u32[]{:S(2)}, u32[]{:S(2)}) collective-permute-start(f32[2,5,32,512]{3,2,1,0:T(8,128)S(1)} %get-tuple-element.90), channel_id=1, source_target_pairs={{0,2},{1,3},{2,4},{3,5},{4,6},{5,7},{6,0},{7,1},{8,10},{9,11},{10,... | collective-permute-start | bytes 1966088 | tf_op jit(solution)/shard_map/ppermute | solution.py:369
  310.7 3.2 collective-permute-start.12
  313.9 17.4 %collective-permute-done.11 = f32[2,5,32,512]{3,2,1,0:T(8,128)S(1)} collective-permute-done((f32[2,5,32,512]{3,2,1,0:T(8,128)S(1)}, f32[2,5,32,512]{3,2,1,0:T(8,128)S(1)}, u32[]{:S(2)}, u32[]{:S(2)}) %collective-permute-start.11) | collective-permute-done | bytes 655392 | tf_op jit(solution)/shard_map/ppermute | solution.py:369
  333.7 27.9 %collective-permute-done.12 = f32[2,5,32,512]{3,2,1,0:T(8,128)S(1)} collective-permute-done((f32[2,5,32,512]{3,2,1,0:T(8,128)S(1)}, f32[2,5,32,512]{3,2,1,0:T(8,128)S(1)}, u32[]{:S(2)}, u32[]{:S(2)}) %collective-permute-start.12) | collective-permute-done | bytes 655392 | tf_op jit(solution)/shard_map/ppermute | solution.py:369
  364.8 2.1 collective-permute-done.14
  369.1 10.5 %all-to-all-done.3.refs_7_ = f32[64,72,256]{2,1,0:T(8,128)} async-done(((f32[64,72,256]{2,1,0:T(8,128)}), f32[64,72,256]{2,1,0:T(8,128)}, u32[]{:S(2)}, u32[]{:S(2)}) %all-to-all-start.3) | async-done | bytes 4718624 | tf_op jit(solution)/shard_map/all_to_all | solution.py:430
  379.6 19.3 %place_and_update.1 = f32[2560,1280]{1,0:T(8,128)} custom-call(s32[141]{0:T(256)S(1)} %concatenate.74.refs_0_, f32[8,10,32,512]{3,2,1,0:T(8,128)} %bitcast.205, f32[256,256]{1,0:T(8,128)S(1)} %copy-done, f32[256,256]{1,0:T(8,128)S(1)} %copy-done.1, f32[8,5,32,512]{3,2,1,0:T(8,128)S(1)} %bitcast.196, f32[64,104,256]{2,1,0:T(8,128)} %all-to-all-done.refs_5_, ...), custom_call_target="tpu_custom_call" | custom-call | flops 10066329600 | bytes 26214400 | tf_op jit(solution)/shard_map/place_and_update/pallas_call | solution.py:302
  (239 shorter events, 81.4 us)
Async XLA Ops:
  6.5 17.1 %copy-start.9 = (s32[32,256]{1,0:T(8,128)S(1)}, s32[32,256]{1,0:T(8,128)}, u32[]{:S(2)}) copy-start(s32[32,256]{1,0:T(8,128)} %param.15) | copy-start | bytes 98308
  6.5 17.7 %copy-start.10 = (s32[32,256]{1,0:T(8,128)S(1)}, s32[32,256]{1,0:T(8,128)}, u32[]{:S(2)}) copy-start(s32[32,256]{1,0:T(8,128)} %param.16) | copy-start | bytes 98308
  6.5 46.5 %all-gather.12.cloned.1.call-start = ((), (), s32[]{:S(2)}) async-start(), calls=%async_computation.6 | async-start | bytes 1474560 | tf_op jit(solution)/shard_map/all_gather | solution.py:425
  7.5 11.2 %collective-permute-start.2 = (f32[512,64]{0,1:T(8,128)S(1)}, f32[512,64]{0,1:T(8,128)S(1)}, u32[]{:S(2)}, u32[]{:S(2)}) collective-permute-start(f32[512,64]{0,1:T(8,128)S(1)} %slice_bitcast_fusion.1), channel_id=1, source_target_pairs={{0,24},{1,25},{2,26},{3,27},{4,28},{5,29},{6,30},{7,31},{32,56},{3... | collective-permute-start | bytes 393224 | tf_op jit(solution)/shard_map/ppermute | solution.py:420
  13.2 5.5 %collective-permute-start.1 = (f32[512,64]{0,1:T(8,128)S(1)}, f32[512,64]{0,1:T(8,128)S(1)}, u32[]{:S(2)}, u32[]{:S(2)}) collective-permute-start(f32[512,64]{0,1:T(8,128)S(1)} %slice_bitcast_fusion.1), channel_id=1, source_target_pairs={{0,16},{1,17},{2,18},{3,19},{4,20},{5,21},{6,22},{7,23},{32,48},{3... | collective-permute-start | bytes 393224 | tf_op jit(solution)/shard_map/ppermute | solution.py:420
  14.5 4.9 %collective-permute-start = (f32[512,64]{0,1:T(8,128)S(1)}, f32[512,64]{0,1:T(8,128)S(1)}, u32[]{:S(2)}, u32[]{:S(2)}) collective-permute-start(f32[512,64]{0,1:T(8,128)S(1)} %slice_bitcast_fusion.1), channel_id=1, source_target_pairs={{0,8},{1,9},{2,10},{3,11},{4,12},{5,13},{6,14},{7,15},{32,40},{33,... | collective-permute-start | bytes 393224 | tf_op jit(solution)/shard_map/ppermute | solution.py:420
  40.3 108.6 %all-to-all-start = ((f32[64,104,256]{2,1,0:T(8,128)}), f32[64,104,256]{2,1,0:T(8,128)}, u32[]{:S(2)}, u32[]{:S(2)}) async-start(f32[64,104,256]{2,1,0:T(8,128)} %get-tuple-element.48), calls=%async_computation | async-start | bytes 13631488 | tf_op jit(solution)/shard_map/all_to_all | solution.py:430
  46.6 77.2 %collective-permute-start.3 = (f32[2,32,32,256]{3,2,1,0:T(8,128)}, f32[2,32,32,256]{3,2,1,0:T(8,128)}, u32[]{:S(2)}, u32[]{:S(2)}) collective-permute-start(f32[2,32,32,256]{3,2,1,0:T(8,128)} %get-tuple-element.44), channel_id=1, source_target_pairs={{0,2},{8,10},{16,18},{24,26},{32,34},{40,42},{48,50},{56,58},{64,6... | collective-permute-start | bytes 6291464 | tf_op jit(solution)/shard_map/ppermute | solution.py:434
  48.6 75.2 %collective-permute-start.4 = (f32[2,32,32,256]{3,2,1,0:T(8,128)}, f32[2,32,32,256]{3,2,1,0:T(8,128)}, u32[]{:S(2)}, u32[]{:S(2)}) collective-permute-start(f32[2,32,32,256]{3,2,1,0:T(8,128)} %get-tuple-element.45), channel_id=1, source_target_pairs={{0,4},{8,12},{16,20},{24,28},{32,36},{40,44},{48,52},{56,60},{64,6... | collective-permute-start | bytes 6291464 | tf_op jit(solution)/shard_map/ppermute | solution.py:434
  50.6 73.3 %collective-permute-start.5 = (f32[2,32,32,256]{3,2,1,0:T(8,128)}, f32[2,32,32,256]{3,2,1,0:T(8,128)}, u32[]{:S(2)}, u32[]{:S(2)}) collective-permute-start(f32[2,32,32,256]{3,2,1,0:T(8,128)} %get-tuple-element.46), channel_id=1, source_target_pairs={{0,6},{8,14},{16,22},{24,30},{32,38},{40,46},{48,54},{56,62},{64,7... | collective-permute-start | bytes 6291464 | tf_op jit(solution)/shard_map/ppermute | solution.py:434
  128.0 10.6 %collective-permute-start.6 = (f32[32,32,256]{2,1,0:T(8,128)S(1)}, f32[32,32,256]{2,1,0:T(8,128)}, u32[]{:S(2)}, u32[]{:S(2)}) collective-permute-start(f32[32,32,256]{2,1,0:T(8,128)S(1)} %slice_bitcast_fusion), channel_id=1, source_target_pairs={{0,1},{2,3},{4,5},{6,7},{8,9},{10,11},{12,13},{14,15},{16,17},{18,... | collective-permute-start | bytes 3145736 | tf_op jit(solution)/shard_map/ppermute | solution.py:436
  152.2 19.8 %collective-permute-start.9 = (f32[2,328,64]{1,2,0:T(8,128)}, f32[2,328,64]{1,2,0:T(8,128)}, u32[]{:S(2)}, u32[]{:S(2)}) collective-permute-start(f32[2,328,64]{1,2,0:T(8,128)} %bitcast.30), channel_id=1, source_target_pairs={{0,6},{1,7},{2,0},{3,1},{4,2},{5,3},{6,4},{7,5},{8,14},{9,15},{10,... | collective-permute-start | bytes 503816 | tf_op jit(solution)/shard_map/ppermute | solution.py:369
  152.4 39.9 %all-to-all-start.1 = ((f32[64,32,256]{2,1,0:T(8,128)}), f32[64,32,256]{2,1,0:T(8,128)S(1)}, u32[]{:S(2)}, u32[]{:S(2)}) async-start(f32[64,32,256]{2,1,0:T(8,128)} %slot_strips.1), calls=%async_computation.1 | async-start | bytes 4194304 | tf_op jit(solution)/shard_map/all_to_all | solution.py:430
  168.4 6.5 %collective-permute-start.8 = (f32[2,328,64]{1,2,0:T(8,128)}, f32[2,328,64]{1,2,0:T(8,128)}, u32[]{:S(2)}, u32[]{:S(2)}) collective-permute-start(f32[2,328,64]{1,2,0:T(8,128)} %bitcast.228), channel_id=1, source_target_pairs={{0,4},{1,5},{2,6},{3,7},{4,0},{5,1},{6,2},{7,3},{8,12},{9,13},{10,... | collective-permute-start | bytes 503816 | tf_op jit(solution)/shard_map/ppermute | solution.py:369
  171.4 6.1 %collective-permute-start.7 = (f32[2,328,64]{1,2,0:T(8,128)S(1)}, f32[2,328,64]{1,2,0:T(8,128)S(1)}, u32[]{:S(2)}, u32[]{:S(2)}) collective-permute-start(f32[2,328,64]{1,2,0:T(8,128)S(1)} %bitcast.229), channel_id=1, source_target_pairs={{0,2},{1,3},{2,4},{3,5},{4,6},{5,7},{6,0},{7,1},{8,10},{9,11},{10,... | collective-permute-start | bytes 503816 | tf_op jit(solution)/shard_map/ppermute | solution.py:369
  177.5 7.6 %collective-permute-start.10 = (f32[4,328,64]{1,2,0:T(8,128)S(1)}, f32[4,328,64]{1,2,0:T(8,128)}, u32[]{:S(2)}, u32[]{:S(2)}) collective-permute-start(f32[4,328,64]{1,2,0:T(8,128)S(1)} %pad_maximum_fusion.6), channel_id=1, source_target_pairs={{0,1},{1,0},{2,3},{3,2},{4,5},{5,4},{6,7},{7,6},{8,9},{9,8},{10,11... | collective-permute-start | bytes 1007624 | tf_op jit(solution)/shard_map/ppermute | solution.py:377
  196.5 94.2 %all-to-all-start.2 = ((f32[64,88,256]{2,1,0:T(8,128)}), f32[64,88,256]{2,1,0:T(8,128)}, u32[]{:S(2)}, u32[]{:S(2)}) async-start(f32[64,88,256]{2,1,0:T(8,128)} %get-tuple-element.57), calls=%async_computation.2 | async-start | bytes 11534336 | tf_op jit(solution)/shard_map/all_to_all | solution.py:430
  203.7 87.0 %all-gather.8.cloned.1.call-start = ((), (), s32[]{:S(2)}) async-start(), calls=%async_computation.4 | async-start | bytes 3276800 | tf_op jit(solution)/shard_map/all_gather | solution.py:486
  204.5 175.2 %all-gather.10.cloned.1.call-start = ((), (), s32[]{:S(2)}) async-start(), calls=%async_computation.5 | async-start | bytes 5898240 | tf_op jit(solution)/shard_map/all_gather | solution.py:490
  290.8 88.8 %all-to-all-start.3 = ((f32[64,72,256]{2,1,0:T(8,128)}), f32[64,72,256]{2,1,0:T(8,128)}, u32[]{:S(2)}, u32[]{:S(2)}) async-start(f32[64,72,256]{2,1,0:T(8,128)} %get-tuple-element.63), calls=%async_computation.3 | async-start | bytes 9437184 | tf_op jit(solution)/shard_map/all_to_all | solution.py:430
  306.2 25.1 %collective-permute-start.11 = (f32[2,5,32,512]{3,2,1,0:T(8,128)S(1)}, f32[2,5,32,512]{3,2,1,0:T(8,128)S(1)}, u32[]{:S(2)}, u32[]{:S(2)}) collective-permute-start(f32[2,5,32,512]{3,2,1,0:T(8,128)S(1)} %get-tuple-element.90), channel_id=1, source_target_pairs={{0,2},{1,3},{2,4},{3,5},{4,6},{5,7},{6,0},{7,1},{8,10},{9,11},{10,... | collective-permute-start | bytes 1966088 | tf_op jit(solution)/shard_map/ppermute | solution.py:369
  310.7 22.2 %collective-permute-start.13 = (f32[2,5,32,512]{3,2,1,0:T(8,128)S(1)}, f32[2,5,32,512]{3,2,1,0:T(8,128)S(1)}, u32[]{:S(2)}, u32[]{:S(2)}) collective-permute-start(f32[2,5,32,512]{3,2,1,0:T(8,128)S(1)} %get-tuple-element.91), channel_id=1, source_target_pairs={{0,6},{1,7},{2,0},{3,1},{4,2},{5,3},{6,4},{7,5},{8,14},{9,15},{10,... | collective-permute-start | bytes 1966088 | tf_op jit(solution)/shard_map/ppermute | solution.py:369
  310.7 50.8 %collective-permute-start.12 = (f32[2,5,32,512]{3,2,1,0:T(8,128)S(1)}, f32[2,5,32,512]{3,2,1,0:T(8,128)S(1)}, u32[]{:S(2)}, u32[]{:S(2)}) collective-permute-start(f32[2,5,32,512]{3,2,1,0:T(8,128)S(1)} %get-tuple-element.92), channel_id=1, source_target_pairs={{0,4},{1,5},{2,6},{3,7},{4,0},{5,1},{6,2},{7,3},{8,12},{9,13},{10,... | collective-permute-start | bytes 1966088 | tf_op jit(solution)/shard_map/ppermute | solution.py:369
  362.5 4.4 %collective-permute-start.14 = (f32[4,5,32,512]{3,2,1,0:T(8,128)S(1)}, f32[4,5,32,512]{3,2,1,0:T(8,128)S(1)}, u32[]{:S(2)}, u32[]{:S(2)}) collective-permute-start(f32[4,5,32,512]{3,2,1,0:T(8,128)S(1)} %pad_maximum_fusion.2), channel_id=1, source_target_pairs={{0,1},{1,0},{2,3},{3,2},{4,5},{5,4},{6,7},{7,6},{8,9},{9,8},{10,11... | collective-permute-start | bytes 3932168 | tf_op jit(solution)/shard_map/ppermute | solution.py:377
  (14 other events, 113.5 us)
Sparse Core Ops, SparseCore 0:
  21.3 26.1 all-gather.11
  206.2 84.5 all-gather.7
  292.4 69.8 all-gather.9
